TPU v7x, 256 devices: a whole 4x4x8 slice. The times are simulated.
256 devices in a mesh: ctx: 32 (over x, z), head: 2 (over y_hi), dp: 4 (over y_lo, core).
Axes of the slice: x: 4, y: 4 (y_hi: 2, y_lo: 2; y = y_hi * 2 + y_lo), z: 8, core: 2. Of those that a mesh axis runs over, the one named last changes fastest.
Arguments:
- tokens: bfloat16 [4, 4096, 8192], P('dp', 'ctx', 'head'), may hold values from -6 to 6
- queries: bfloat16 [4, 4096, 4096], P('dp', 'ctx', 'head'), may hold values from -120 to 120
- out_grad: bfloat16 [4, 4096, 4096], P('dp', 'ctx', 'head'), may hold values from -6 to 6
- key_weight: bfloat16 [8192, 512], P(None, 'head'), may hold values from -0.0625 to 0.0625
- value_weight: bfloat16 [8192, 512], P(None, 'head'), may hold values from -0.0625 to 0.0625
- noise_codes: int32 [2, 4, 4096, 512], P(None, 'dp', 'ctx', 'head'), may hold values from 0 to 15
- clip_masks: int32 [2, 4, 4096, 512], P(None, 'dp', 'ctx', 'head'), may hold values 0 or 1
- block_order: int32 [32], replicated, may hold values from 0 to 31, each once
Outputs:
- query_grad: bfloat16 [4, 4096, 4096], P('dp', 'ctx', 'head')
- key_weight_grad: float32 [8192, 512], P('ctx', 'head')
- value_weight_grad: float32 [8192, 512], P('ctx', 'head')
Inputs may be any that keep to these rules, and one draw needn't show every extreme that they name: `block_order`: each block place appears once.
All inputs are finite; a program needn't handle non-finite values. No bound on the sum of `clip_masks` on one device may be relied on, other than what follows from the above.
Results may differ from a plain program's by a relative error of at most 0.029.
The roundings to bfloat16 on the way count: a program that leaves them out, or rounds other values in their place, can miss the bound.
Values may be sent and summed in bfloat16 or wider, within the bound.
A program may use at most 128 MiB of HBM per device.

v0:
```python
import math

import jax
import jax.numpy as jnp
from jax import lax
from jax.sharding import PartitionSpec as P

HD = 128
GROUP = 8


NOISE_STEP = 0.05
NOISE_MIDDLE = 7.5
FLOOR_SCORE = -1e30


def from_behind(array, axis, by):
    count = lax.axis_size(axis)
    return lax.ppermute(array, axis, [(i, (i + by) % count) for i in range(count)])


def pick_entry(table, wanted):
    spots = jnp.arange(table.shape[0], dtype=jnp.int32)
    return jnp.sum(jnp.where(spots == wanted, table, 0))


def project(features, weight, codes):
    before = jnp.dot(features, weight, preferred_element_type=jnp.float32)
    return (before + NOISE_STEP * (codes.astype(jnp.float32) - NOISE_MIDDLE)).astype(jnp.bfloat16)


def block_scores(query_heads, key_block, score_scale, query_places, key_places):
    scores = (
        jnp.einsum("qjgd,kjd->jgqk", query_heads, key_block, preferred_element_type=jnp.float32)
        * score_scale
    )
    return jnp.where(query_places[:, None] >= key_places[None, :], scores, FLOOR_SCORE)


def on_device(
    tokens, queries, out_grad, key_weight, value_weight, noise_codes, clip_masks, block_order
):
    token_count = queries.shape[1]
    kv_width = key_weight.shape[1]
    kv_local = kv_width // HD
    cycle_size = lax.axis_size("ctx")
    cycle_index = lax.axis_index("ctx")
    score_scale = 1.0 / math.sqrt(HD)
    whole_x = lax.all_gather(tokens[0], "head", axis=1, tiled=True)
    keys = project(whole_x, key_weight, noise_codes[0, 0])
    values = project(whole_x, value_weight, noise_codes[1, 0])
    local_kv = jnp.stack([keys, values], axis=1)
    all_kv = lax.all_gather(local_kv, "ctx", axis=0, tiled=True)
    offsets = jnp.arange(token_count, dtype=jnp.int32)
    my_place = pick_entry(block_order, cycle_index)
    query_places = my_place * token_count + offsets
    query_heads = queries[0].reshape(token_count, kv_local, GROUP, HD)
    grad_heads = out_grad[0].reshape(token_count, kv_local, GROUP, HD)

    def block_kv(block_index):
        piece = lax.dynamic_slice_in_dim(all_kv, block_index * token_count, token_count, 0)
        key_block = piece[:, 0].reshape(token_count, kv_local, HD)
        value_block = piece[:, 1].reshape(token_count, kv_local, HD)
        return (key_block, value_block, pick_entry(block_order, block_index))

    def stats_step(block_index, carry):
        key_block, value_block, block_place = block_kv(block_index)

        def live(state):
            old_max, old_total, old_weighted = state
            scores = block_scores(
                query_heads,
                key_block,
                score_scale,
                query_places,
                block_place * token_count + offsets,
            )
            new_max = jnp.maximum(old_max, jnp.max(scores, axis=-1))
            rescale = jnp.exp(old_max - new_max)
            weights = jnp.exp(scores - new_max[..., None])
            prob_grad = jnp.einsum(
                "qjgd,kjd->jgqk", grad_heads, value_block, preferred_element_type=jnp.float32
            )
            new_total = old_total * rescale + jnp.sum(weights, axis=-1)
            new_weighted = old_weighted * rescale + jnp.sum(weights * prob_grad, axis=-1)
            return (new_max, new_total, new_weighted)

        return lax.cond(block_place <= my_place, live, lambda state: state, carry)

    stat_shape = (kv_local, GROUP, token_count)
    start_state = (
        jnp.full(stat_shape, FLOOR_SCORE, jnp.float32),
        jnp.zeros(stat_shape, jnp.float32),
        jnp.zeros(stat_shape, jnp.float32),
    )
    row_max, row_total, row_weighted = lax.fori_loop(0, cycle_size, stats_step, start_state)
    log_total = row_max + jnp.log(row_total)
    deltas = row_weighted / row_total
    zero_query = jnp.zeros((token_count, kv_local, GROUP, HD), jnp.float32)
    zero_pair = jnp.zeros((token_count, 2, kv_width), jnp.float32)

    def block_grads(operands):
        key_block, value_block, block_place = operands
        scores = block_scores(
            query_heads, key_block, score_scale, query_places, block_place * token_count + offsets
        )
        probs = jnp.exp(scores - log_total[..., None])
        prob_grad = jnp.einsum(
            "qjgd,kjd->jgqk", grad_heads, value_block, preferred_element_type=jnp.float32
        )
        score_grad = (probs * (prob_grad - deltas[..., None])).astype(jnp.bfloat16)
        probs_low = probs.astype(jnp.bfloat16)
        query_add = (
            jnp.einsum("jgqk,kjd->qjgd", score_grad, key_block, preferred_element_type=jnp.float32)
            * score_scale
        )
        key_add = (
            jnp.einsum(
                "jgqk,qjgd->kjd", score_grad, query_heads, preferred_element_type=jnp.float32
            )
            * score_scale
        )
        value_add = jnp.einsum(
            "jgqk,qjgd->kjd", probs_low, grad_heads, preferred_element_type=jnp.float32
        )
        pair_add = jnp.stack(
            [key_add.reshape(token_count, kv_width), value_add.reshape(token_count, kv_width)],
            axis=1,
        )
        return (query_add, pair_add)

    def maybe_grads(block_index):
        key_block, value_block, block_place = block_kv(block_index)
        return lax.cond(
            block_place <= my_place,
            block_grads,
            lambda operands: (zero_query, zero_pair),
            (key_block, value_block, block_place),
        )

    def cycle_step(step_index, carry):
        query_sum, travel = carry
        block_index = (cycle_index - step_index) % cycle_size
        query_add, pair_add = maybe_grads(block_index)
        travel = from_behind(travel + pair_add, "ctx", 1)
        return (query_sum + query_add, travel)

    query_sum, own_grads = lax.fori_loop(0, cycle_size, cycle_step, (zero_query, zero_pair))
    clip_factor = jnp.transpose(clip_masks[:, 0], (1, 0, 2)).astype(jnp.float32)
    pre_grads = (own_grads * clip_factor).astype(jnp.bfloat16)
    flat_grads = pre_grads.reshape(token_count, 2 * kv_width)
    contract = (((0,), (0,)), ((), ()))
    weight_part = lax.psum_scatter(
        lax.dot_general(whole_x, flat_grads, contract, preferred_element_type=jnp.float32).astype(
            jnp.bfloat16
        ),
        "ctx",
        scatter_dimension=0,
        tiled=True,
    )
    weight_sum = lax.psum(weight_part, "dp").astype(jnp.float32) / lax.axis_size("dp")
    query_out = query_sum.astype(jnp.bfloat16).reshape(1, token_count, kv_local * GROUP * HD)
    return (query_out, weight_sum[:, :kv_width], weight_sum[:, kv_width:])


def solution(mesh):
    placed = (
        P("dp", "ctx", "head"),
        P("dp", "ctx", "head"),
        P("dp", "ctx", "head"),
        P(None, "head"),
        P(None, "head"),
        P(None, "dp", "ctx", "head"),
        P(None, "dp", "ctx", "head"),
        P(),
    )
    return jax.shard_map(
        on_device,
        mesh=mesh,
        in_specs=placed,
        out_specs=(P("dp", "ctx", "head"), P("ctx", "head"), P("ctx", "head")),
        check_vma=False,
    )
```

profile of v0, /device:TPU:71, one launch (start us, length us, event | category | flops | bytes accessed | tf_op | source)
XLA Modules:
  0.0 1124.7 jit_solution(8964840964205400547)
XLA Ops:
  8.0 43.8 %all-gather.6.cloned.1.call-done = bf16[1,128,8192]{2,1,0:T(8,128)(2,1)} async-done(((bf16[1,128,4096]{2,1,0:T(8,128)(2,1)}), bf16[1,128,8192]{2,1,0:T(8,128)(2,1)}) %all-gather.6.cloned.1.call-update) | async-done | bytes 2097168 | tf_op jit(solution)/shard_map/all_gather | solution.py:49
  62.3 71.8 %all-gather.4.cloned.1.call-done = bf16[4096,2,256]{2,0,1:T(8,128)(2,1)} async-done(((bf16[128,2,256]{2,0,1:T(8,128)(2,1)}), bf16[4096,2,256]{2,0,1:T(8,128)(2,1)}) %all-gather.4.cloned.1.call-update) | async-done | bytes 4194320 | tf_op jit(solution)/shard_map/all_gather | solution.py:53
  134.1 6.4 copy.41
  140.5 106.8 %while.36 = (s32[]{:T(128)}, f32[2,8,128]{2,1,0:T(8,128)S(1)}, f32[2,8,128]{2,1,0:T(8,128)S(1)}, f32[2,8,128]{2,1,0:T(8,128)S(1)}, s32[32]{0:T(128)S(1)}, /*inde...) while((s32[]{:T(128)}, f32[2,8,128]{2,1,0:T(8,128)S(1)}, ...), condition=%wide.region_8.9_spmd.clone, body=%wide.region_1.8_spmd.clone.sunk | while | flops 136337760 | bytes 4771825 | solution.py:96
  248.1 527.8 %while.37 = (s32[]{:T(128)}, f32[128,2,8,128]{3,0,2,1:T(8,128)S(1)}, f32[128,2,256]{0,2,1:T(8,128)}, s32[]{:T(128)}, s32[32]{0:T(128)S(1)}, /*index=5*/s32[]{:T(...) while((s32[]{:T(128)}, ...), condition=%wide.region_13.14_spmd.clone, body=%wide.region_9.13_spmd.clone.sunk | while | flops 338346336 | bytes 15192232 | solution.py:148
  255.3 34.4 %collective-permute-start = (f32[128,2,256]{0,2,1:T(8,128)}, f32[128,2,256]{0,2,1:T(8,128)S(1)}, u32[]{:S(2)}, u32[]{:S(2)}) collective-permute-start(f32[128,2,256]{0,2,1:T(8,128)} %add.206), channel_id=1, source_target_pairs={{0,8},{8,16},{16,24},{24,32},{32,40},{40,48},{48,56},{56,64},{64,7... | collective-permute-start | bytes 786440 | tf_op jit(solution)/shard_map/while/body/eval_jaxpr/ppermute | solution.py:19
  297.9 5.1 collective-permute-start
  311.3 5.1 collective-permute-start
  352.0 6.4 collective-permute-start
  401.6 5.8 collective-permute-done
  417.8 5.0 collective-permute-done
  496.0 5.5 collective-permute-done
  519.5 5.3 collective-permute-start
  533.0 8.8 collective-permute-start
  550.0 7.4 collective-permute-start
  569.4 5.1 collective-permute-done
  579.0 9.0 collective-permute-start
  613.3 8.5 collective-permute-start
  629.9 5.1 collective-permute-start
  646.7 11.8 %collective-permute-start = (f32[128,2,256]{0,2,1:T(8,128)}, f32[128,2,256]{0,2,1:T(8,128)S(1)}, u32[]{:S(2)}, u32[]{:S(2)}) collective-permute-start(f32[128,2,256]{0,2,1:T(8,128)} %add.206), channel_id=1, source_target_pairs={{0,8},{8,16},{16,24},{24,32},{32,40},{40,48},{48,56},{56,64},{64,7... | collective-permute-start | bytes 786440 | tf_op jit(solution)/shard_map/while/body/eval_jaxpr/ppermute | solution.py:19
  681.2 8.2 collective-permute-start
  689.8 5.0 collective-permute-done
  699.4 6.6 collective-permute-start
  706.4 4.9 collective-permute-done
  716.0 7.2 collective-permute-start
  723.5 4.9 collective-permute-done
  733.0 5.4 collective-permute-start
  746.6 11.6 %collective-permute-start = (f32[128,2,256]{0,2,1:T(8,128)}, f32[128,2,256]{0,2,1:T(8,128)S(1)}, u32[]{:S(2)}, u32[]{:S(2)}) collective-permute-start(f32[128,2,256]{0,2,1:T(8,128)} %add.206), channel_id=1, source_target_pairs={{0,8},{8,16},{16,24},{24,32},{32,40},{40,48},{48,56},{56,64},{64,7... | collective-permute-start | bytes 786440 | tf_op jit(solution)/shard_map/while/body/eval_jaxpr/ppermute | solution.py:19
  766.4 5.1 collective-permute-start
  777.0 7.1 fusion.26
  784.2 282.7 %reduce-scatter.2.cloned.1.call-done = bf16[256,512]{0,1:T(8,128)(2,1)} async-done(((bf16[8192,512]{0,1:T(8,128)(2,1)}), bf16[256,512]{0,1:T(8,128)(2,1)}) %reduce-scatter.2.cloned.1.call-update) | async-done | bytes 262160 | tf_op jit(solution)/shard_map/reduce_scatter | solution.py:153
  1068.4 47.1 %all-reduce.2.cloned.1.call-done = bf16[256,512]{0,1:T(8,128)(2,1)} async-done(((bf16[256,512]{0,1:T(8,128)(2,1)}), bf16[256,512]{0,1:T(8,128)(2,1)}) %all-reduce.2.cloned.1.call-update) | async-done | bytes 262160 | tf_op jit(solution)/shard_map/psum | solution.py:161
  (755 shorter events, 465.0 us)
Async XLA Ops:
  7.2 44.6 %all-gather.6.cloned.1.call-start = ((), (), s32[]{:S(2)}) async-start(), calls=%async_computation.4 | async-start | bytes 3145728 | tf_op jit(solution)/shard_map/all_gather | solution.py:49
  7.9 126.2 %all-gather.4.cloned.1.call-start = ((), (), s32[]{:S(2)}) async-start(), calls=%async_computation.1 | async-start | bytes 4325376 | tf_op jit(solution)/shard_map/all_gather | solution.py:53
  57.9 1008.9 %reduce-scatter.2.cloned.1.call-start = ((), (), s32[]{:S(2)}) async-start(), calls=%async_computation.2 | async-start | bytes 8650752 | tf_op jit(solution)/shard_map/reduce_scatter | solution.py:153
  255.3 38.0 %collective-permute-start = (f32[128,2,256]{0,2,1:T(8,128)}, f32[128,2,256]{0,2,1:T(8,128)S(1)}, u32[]{:S(2)}, u32[]{:S(2)}) collective-permute-start(f32[128,2,256]{0,2,1:T(8,128)} %add.206), channel_id=1, source_target_pairs={{0,8},{8,16},{16,24},{24,32},{32,40},{40,48},{48,56},{56,64},{64,7... | collective-permute-start | bytes 786440 | tf_op jit(solution)/shard_map/while/body/eval_jaxpr/ppermute | solution.py:19
  297.9 8.8 collective-permute-start
  311.3 8.8 collective-permute-start
  341.4 6.0 collective-permute-start
  352.0 10.0 collective-permute-start
  369.9 6.6 collective-permute-start
  384.5 6.6 collective-permute-start
  399.1 8.4 collective-permute-start
  415.4 7.4 collective-permute-start
  430.7 6.5 collective-permute-start
  445.1 9.2 collective-permute-start
  462.3 7.3 collective-permute-start
  477.5 6.9 collective-permute-start
  492.4 9.1 collective-permute-start
  519.5 9.0 collective-permute-start
  533.0 12.4 %collective-permute-start = (f32[128,2,256]{0,2,1:T(8,128)}, f32[128,2,256]{0,2,1:T(8,128)S(1)}, u32[]{:S(2)}, u32[]{:S(2)}) collective-permute-start(f32[128,2,256]{0,2,1:T(8,128)} %add.206), channel_id=1, source_target_pairs={{0,8},{8,16},{16,24},{24,32},{32,40},{40,48},{48,56},{56,64},{64,7... | collective-permute-start | bytes 786440 | tf_op jit(solution)/shard_map/while/body/eval_jaxpr/ppermute | solution.py:19
  550.0 11.0 collective-permute-start
  579.0 12.7 %collective-permute-start = (f32[128,2,256]{0,2,1:T(8,128)}, f32[128,2,256]{0,2,1:T(8,128)S(1)}, u32[]{:S(2)}, u32[]{:S(2)}) collective-permute-start(f32[128,2,256]{0,2,1:T(8,128)} %add.206), channel_id=1, source_target_pairs={{0,8},{8,16},{16,24},{24,32},{32,40},{40,48},{48,56},{56,64},{64,7... | collective-permute-start | bytes 786440 | tf_op jit(solution)/shard_map/while/body/eval_jaxpr/ppermute | solution.py:19
  613.3 12.1 %collective-permute-start = (f32[128,2,256]{0,2,1:T(8,128)}, f32[128,2,256]{0,2,1:T(8,128)S(1)}, u32[]{:S(2)}, u32[]{:S(2)}) collective-permute-start(f32[128,2,256]{0,2,1:T(8,128)} %add.206), channel_id=1, source_target_pairs={{0,8},{8,16},{16,24},{24,32},{32,40},{40,48},{48,56},{56,64},{64,7... | collective-permute-start | bytes 786440 | tf_op jit(solution)/shard_map/while/body/eval_jaxpr/ppermute | solution.py:19
  629.9 8.8 collective-permute-start
  646.7 15.4 %collective-permute-start = (f32[128,2,256]{0,2,1:T(8,128)}, f32[128,2,256]{0,2,1:T(8,128)S(1)}, u32[]{:S(2)}, u32[]{:S(2)}) collective-permute-start(f32[128,2,256]{0,2,1:T(8,128)} %add.206), channel_id=1, source_target_pairs={{0,8},{8,16},{16,24},{24,32},{32,40},{40,48},{48,56},{56,64},{64,7... | collective-permute-start | bytes 786440 | tf_op jit(solution)/shard_map/while/body/eval_jaxpr/ppermute | solution.py:19
  670.0 6.6 collective-permute-start
  681.2 13.6 %collective-permute-start = (f32[128,2,256]{0,2,1:T(8,128)}, f32[128,2,256]{0,2,1:T(8,128)S(1)}, u32[]{:S(2)}, u32[]{:S(2)}) collective-permute-start(f32[128,2,256]{0,2,1:T(8,128)} %add.206), channel_id=1, source_target_pairs={{0,8},{8,16},{16,24},{24,32},{32,40},{40,48},{48,56},{56,64},{64,7... | collective-permute-start | bytes 786440 | tf_op jit(solution)/shard_map/while/body/eval_jaxpr/ppermute | solution.py:19
  699.4 11.9 %collective-permute-start = (f32[128,2,256]{0,2,1:T(8,128)}, f32[128,2,256]{0,2,1:T(8,128)S(1)}, u32[]{:S(2)}, u32[]{:S(2)}) collective-permute-start(f32[128,2,256]{0,2,1:T(8,128)} %add.206), channel_id=1, source_target_pairs={{0,8},{8,16},{16,24},{24,32},{32,40},{40,48},{48,56},{56,64},{64,7... | collective-permute-start | bytes 786440 | tf_op jit(solution)/shard_map/while/body/eval_jaxpr/ppermute | solution.py:19
  716.0 12.4 %collective-permute-start = (f32[128,2,256]{0,2,1:T(8,128)}, f32[128,2,256]{0,2,1:T(8,128)S(1)}, u32[]{:S(2)}, u32[]{:S(2)}) collective-permute-start(f32[128,2,256]{0,2,1:T(8,128)} %add.206), channel_id=1, source_target_pairs={{0,8},{8,16},{16,24},{24,32},{32,40},{40,48},{48,56},{56,64},{64,7... | collective-permute-start | bytes 786440 | tf_op jit(solution)/shard_map/while/body/eval_jaxpr/ppermute | solution.py:19
  733.0 9.1 collective-permute-start
  746.6 15.2 %collective-permute-start = (f32[128,2,256]{0,2,1:T(8,128)}, f32[128,2,256]{0,2,1:T(8,128)S(1)}, u32[]{:S(2)}, u32[]{:S(2)}) collective-permute-start(f32[128,2,256]{0,2,1:T(8,128)} %add.206), channel_id=1, source_target_pairs={{0,8},{8,16},{16,24},{24,32},{32,40},{40,48},{48,56},{56,64},{64,7... | collective-permute-start | bytes 786440 | tf_op jit(solution)/shard_map/while/body/eval_jaxpr/ppermute | solution.py:19
  766.4 8.8 collective-permute-start
  784.1 331.3 %all-reduce.2.cloned.1.call-start = ((), (), s32[]{:S(2)}) async-start(), calls=%async_computation.3 | async-start | bytes 524288 | tf_op jit(solution)/shard_map/psum | solution.py:161
  (42 other events, 112.9 us)
Sparse Core Ops, SparseCore 0:
  9.8 41.8 all-gather.5
  58.1 75.9 all-gather.3
  784.3 282.5 reduce-scatter.1
  1069.5 45.8 all-reduce.1
where the time goes:
time: 1130 us; the launch traced here: 1120 us
  waiting for transfers between devices  568 us (50%)
  starting transfers between devices  188 us (17%)
  other arithmetic  118 us (10%)
  loops' own time  110 us (10%)
  local copies, waits for them, and re-layouts  70.4 us (6%)
  matrix products  55.5 us (5%)
  between operations  14.5 us (1%)
    reduce_scatter x1, waiting for transfers between devices, on_device(): lax.psum_scatter(lax.dot_general(whole_x, flat_grads, contract, preferred...  283 us
    ppermute x32, starting transfers between devices, from_behind(): lax.ppermute(array, axis, [(i, (i + by) % count) for i in range(count)])  188 us
    ppermute x32, waiting for transfers between devices, from_behind(): lax.ppermute(array, axis, [(i, (i + by) % count) for i in range(count)])  122 us
    all_gather x1, waiting for transfers between devices, on_device(): all_kv = lax.all_gather(local_kv, 'ctx', axis=0, tiled=True)  71.8 us
    add x32, other arithmetic, cycle_step(): travel = from_behind(travel + pair_add, 'ctx', 1)  53.9 us
    psum x1, waiting for transfers between devices, on_device(): lax.psum(weight_part, 'dp').astype(jnp.float32) / lax.axis_size('dp')  47.1 us
    reduce_sum x65, other arithmetic, pick_entry(): return jnp.sum(jnp.where(spots == wanted, table, 0))  43.9 us
    all_gather x1, waiting for transfers between devices, on_device(): whole_x = lax.all_gather(tokens[0], 'head', axis=1, tiled=True)  43.8 us
  transfers between devices with their start and end apart: 36, of which 36 were waited for; matrix products, arithmetic and copies ran while one was open for 1% of the time, Pallas kernels for 0%

commit v1 on v0

v1 whole, which is shorter than its diff:
```python
import functools
import math

import jax
import jax.numpy as jnp
from jax import lax
from jax.experimental import pallas as pl
from jax.experimental.pallas import tpu as pltpu
from jax.sharding import PartitionSpec as P

HD = 128
BLK = 128
NX, NY, NZ, NC = 4, 4, 8, 2
GROUP_COLS = 512
HALF_D = 4096
QUARTER = 1024
KV_W = 256
BLOCKS = 32
NOISE_STEP = 0.05
NOISE_MIDDLE = 7.5
SCALE = 1.0 / math.sqrt(HD)
SCALE_LOG2 = SCALE * math.log2(math.e)
FLOOR_SCORE = -1e30
BF = jnp.bfloat16
F32 = jnp.float32
MESH = pl.DeviceIdType.MESH
NT = (((1,), (1,)), ((), ()))
NN = (((1,), (0,)), ((), ()))
TN = (((0,), (0,)), ((), ()))


def here():
    ctx, head, dp = lax.axis_index("ctx"), lax.axis_index("head"), lax.axis_index("dp")
    return ctx // NZ, head * 2 + dp // 2, lax.rem(ctx, NZ), lax.rem(dp, 2)


def device(x, y, z, core):
    return {"ctx": x * NZ + z, "head": y // 2, "dp": lax.rem(y, 2) * 2 + core}


def around(value, count):
    return lax.rem(value + count, count)


def signal(target):
    pl.semaphore_signal(pltpu.get_barrier_semaphore(), inc=1, device_id=target, device_id_type=MESH)


def remote(src, dst, send_sem, recv_sem, target):
    return pltpu.make_async_remote_copy(
        src_ref=src, dst_ref=dst, send_sem=send_sem, recv_sem=recv_sem, device_id=target, device_id_type=MESH
    )


def wait_bytes(ref, sem):
    pltpu.make_async_copy(ref, ref, sem).wait()


def send_or_copy(is_self, src, dst, send_sem, recv_sem, target):
    @pl.when(is_self)
    def _():
        pltpu.make_async_copy(src, dst, recv_sem).start()

    @pl.when(jnp.logical_not(is_self))
    def _():
        remote(src, dst, send_sem, recv_sem, target).start()


def wait_sent(is_self, ref, send_sem):
    @pl.when(jnp.logical_not(is_self))
    def _():
        wait_bytes(ref, send_sem)


ROW_CHUNKS = 4
CHUNK = BLK // ROW_CHUNKS


def front_kernel(
    tok, q, do, kw, vw, codes, qx, dox, kv,
    xbuf, wbuf, acc, kvst,
    w_sem, own_sem, tok_send, tok_recv, q_send, q_recv, kv_send, kv_send0, kv_recv, fw_send, fw_recv,
):
    X, Y, Z, C = here()
    head = Y // 2
    unit_core = X // 2
    same = unit_core == C
    peer = device(X, around(Y + 2, NY), Z, C)
    partner = device(X, Y, Z, 1 - C)

    loads = []
    for half in range(2):
        rows = pl.ds(half * HALF_D, HALF_D)
        loads.append(pltpu.make_async_copy(kw.at[rows, :], wbuf.at[half, :, pl.ds(0, KV_W)], w_sem.at[half, 0]))
        loads.append(pltpu.make_async_copy(vw.at[rows, :], wbuf.at[half, :, pl.ds(KV_W, KV_W)], w_sem.at[half, 1]))
    own_x = pltpu.make_async_copy(tok.at[0], xbuf.at[head], own_sem)
    own_x.start()
    for load in loads:
        load.start()

    signal(peer)
    signal(partner)
    for xs in range(NX):
        @pl.when(jnp.logical_not(jnp.logical_and(same, X == xs)))
        def _(xs=xs):
            signal(device(xs, Y, Z, unit_core))
    for part in range(2):
        signal_x = 2 * C + part

        @pl.when(jnp.logical_not(jnp.logical_and(same, X == signal_x)))
        def _(signal_x=signal_x):
            signal(device(signal_x, Y, Z, unit_core))

        def far(step, carry, signal_x=signal_x):
            signal(device(signal_x, Y, around(Z + step, NZ), unit_core))
            return carry

        lax.fori_loop(1, NZ, far, 0)
    pl.semaphore_wait(pltpu.get_barrier_semaphore(), 22 - 2 * same.astype(jnp.int32))

    for r in range(ROW_CHUNKS):
        rows = pl.ds(r * CHUNK, CHUNK)
        remote(tok.at[0, rows, :], xbuf.at[head, rows, :], tok_send.at[r], tok_recv.at[r], peer).start()
    for j in range(2):
        for c2 in range(NC):
            cols = pl.ds((j * 8 + c2 * 4) * HD, GROUP_COLS)
            target = device(2 * C + j, Y, Z, c2)
            is_self = jnp.logical_and(2 * C + j == X, C == c2)
            send_or_copy(is_self, q.at[0, :, cols], qx.at[X], q_send.at[0, j, c2], q_recv.at[0], target)
            send_or_copy(is_self, do.at[0, :, cols], dox.at[X], q_send.at[1, j, c2], q_recv.at[1], target)

    own_x.wait()
    for load in loads:
        load.wait()
    acc[...] = jnp.dot(xbuf[head], wbuf[head], preferred_element_type=F32)

    mine = X * NZ + Z

    def forward(r):
        rows = pl.ds(r * CHUNK, CHUNK)
        blocks = kv.at[pl.ds(C * 16, 16), rows, :]
        wait_bytes(blocks, kv_recv.at[r])
        copy = remote(blocks, blocks, fw_send.at[r], fw_recv.at[r], partner)
        copy.start()

    for r in range(ROW_CHUNKS):
        rows = pl.ds(r * CHUNK, CHUNK)
        wait_bytes(xbuf.at[1 - head, rows, :], tok_recv.at[r])
        both = acc[rows, :] + jnp.dot(xbuf[1 - head, rows, :], wbuf[1 - head], preferred_element_type=F32)
        for what in range(2):
            shift = NOISE_STEP * (codes[what, 0, rows, :].astype(F32) - NOISE_MIDDLE)
            value = (both[:, what * KV_W : (what + 1) * KV_W] + shift).astype(BF)
            for j in range(2):
                kvst[j, rows, what * HD : (what + 1) * HD] = value[:, j * HD : (j + 1) * HD]
        for j in range(2):
            src = kvst.at[j, rows, :]
            dst = kv.at[mine, rows, :]
            is_self = jnp.logical_and(same, 2 * C + j == X)
            send_or_copy(is_self, src, dst, kv_send0.at[r, j], kv_recv.at[r], device(2 * C + j, Y, Z, unit_core))

            def far(step, carry, j=j, r=r, src=src, dst=dst):
                target = device(2 * C + j, Y, around(Z + step, NZ), unit_core)
                remote(src, dst, kv_send.at[r, j], kv_recv.at[r], target).start()
                return carry

            lax.fori_loop(1, NZ, far, 0)
        if r:
            forward(r - 1)
    forward(ROW_CHUNKS - 1)

    for r in range(ROW_CHUNKS):
        rows = pl.ds(r * CHUNK, CHUNK)
        wait_bytes(kv.at[pl.ds((1 - C) * 16, 16), rows, :], fw_recv.at[r])
        wait_bytes(kv.at[pl.ds(C * 16, 16), rows, :], fw_send.at[r])
        wait_bytes(xbuf.at[head, rows, :], tok_send.at[r])
        for j in range(2):
            is_self = jnp.logical_and(same, 2 * C + j == X)
            wait_sent(is_self, kvst.at[j, rows, :], kv_send0.at[r, j])
            wait_bytes(kv.at[pl.ds(0, NZ - 1), rows, :], kv_send.at[r, j])
    wait_bytes(qx, q_recv.at[0])
    wait_bytes(dox, q_recv.at[1])
    for j in range(2):
        for c2 in range(NC):
            is_self = jnp.logical_and(2 * C + j == X, C == c2)
            wait_sent(is_self, qx.at[0], q_send.at[0, j, c2])
            wait_sent(is_self, dox.at[0], q_send.at[1, j, c2])


ANY_SPEC = pl.BlockSpec(memory_space=pl.ANY)
VMEM_SPEC = pl.BlockSpec(memory_space=pltpu.VMEM)
DMA = pltpu.SemaphoreType.DMA


def front(tokens, queries, out_grad, key_weight, value_weight, noise_codes):
    return pl.pallas_call(
        front_kernel,
        name="front",
        out_shape=(
            jax.ShapeDtypeStruct((NX, BLK, GROUP_COLS), BF),
            jax.ShapeDtypeStruct((NX, BLK, GROUP_COLS), BF),
            jax.ShapeDtypeStruct((BLOCKS, BLK, KV_W), BF),
        ),
        in_specs=[ANY_SPEC] * 5 + [VMEM_SPEC],
        out_specs=(ANY_SPEC,) * 3,
        scratch_shapes=[
            pltpu.VMEM((2, BLK, HALF_D), BF),
            pltpu.VMEM((2, HALF_D, 2 * KV_W), BF),
            pltpu.VMEM((BLK, 2 * KV_W), F32),
            pltpu.VMEM((2, BLK, KV_W), BF),
            DMA((2, 2)),
            DMA,
            DMA((ROW_CHUNKS,)),
            DMA((ROW_CHUNKS,)),
            DMA((2, 2, 2)),
            DMA((2,)),
            DMA((ROW_CHUNKS, 2)),
            DMA((ROW_CHUNKS, 2)),
            DMA((ROW_CHUNKS,)),
            DMA((ROW_CHUNKS,)),
            DMA((ROW_CHUNKS,)),
        ],
        compiler_params=pltpu.CompilerParams(
            collective_id=0, has_side_effects=True, vmem_limit_bytes=40 * 2**20
        ),
        cost_estimate=pl.CostEstimate(flops=10**9, bytes_accessed=16 * 2**20, transcendentals=0),
    )(tokens, queries, out_grad, key_weight, value_weight, noise_codes)


KEYS = 256
LEVELS = (4, 2, 1)
ROWS = 4 * BLK


def attention_kernel(
    order, q, do, kv, dq_out, dkv_out,
    kvb, qs, dos, stb, dpb, dk, dv, dqt, dkvb, kv_sem, q_sem, do_sem, out_sem,
):
    Z = lax.rem(lax.axis_index("ctx"), NZ)

    def at_place(block):
        return pl.ds(pl.multiple_of(order[block] * BLK, BLK), BLK)

    def load(block, carry):
        pltpu.make_async_copy(kv.at[block], kvb.at[at_place(block), :], kv_sem).start()
        return carry

    for x in range(NX):
        for h in range(4):
            cols, rows = pl.ds(h * HD, HD), pl.ds(h * BLK, BLK)
            pltpu.make_async_copy(q.at[x, :, cols], qs.at[x, rows, :], q_sem).start()
            pltpu.make_async_copy(do.at[x, :, cols], dos.at[x, rows, :], do_sem).start()
    lax.fori_loop(0, BLOCKS, load, 0)

    def clear(i, carry):
        rows = pl.ds(pl.multiple_of(i * 256, 256), 256)
        dk[rows, :] = jnp.zeros((256, HD), F32)
        dv[rows, :] = jnp.zeros((256, HD), F32)
        return carry

    lax.fori_loop(0, 16, clear, 0)
    wait_bytes(qs, q_sem)
    wait_bytes(dos, do_sem)
    wait_bytes(kvb, kv_sem)

    def run(count, body, carry):
        done = 0
        for units in LEVELS:
            times = (count - done) // units
            base = done

            def step(i, state, units=units, base=base):
                start = pl.multiple_of((base + i * units) * KEYS, KEYS)
                return body(pl.ds(start, units * KEYS), units * KEYS, state)

            carry = lax.fori_loop(0, times, step, carry)
            done = base + times * units
        return carry

    def fold(array, size, how):
        return how(array.reshape(size // 8, 8, ROWS), axis=0)

    def tile(x, carry):
        place = order[x * NZ + Z]
        last = place // 2
        qx = qs[x]
        dx = dos[x]

        def score_step(rows, size, top):
            st = lax.dot_general(kvb[rows, :HD], qx, NT, preferred_element_type=F32)
            stb[rows, :] = st
            return jnp.maximum(top, fold(st, size, jnp.max))

        top = run(last, score_step, jnp.full((8, ROWS), FLOOR_SCORE, F32))
        rows = pl.ds(pl.multiple_of(last * KEYS, KEYS), KEYS)
        st = lax.dot_general(kvb[rows, :HD], qx, NT, preferred_element_type=F32)
        key_places = last * KEYS + lax.broadcasted_iota(jnp.int32, (KEYS, ROWS), 0)
        query_places = place * BLK + lax.rem(lax.broadcasted_iota(jnp.int32, (KEYS, ROWS), 1), BLK)
        st = jnp.where(key_places <= query_places, st, FLOOR_SCORE)
        stb[rows, :] = st
        top = jnp.maximum(top, fold(st, KEYS, jnp.max))
        top = jnp.max(top, axis=0, keepdims=True) * SCALE_LOG2

        def weigh_step(rows, size, state):
            total, weighted = state
            weights = jnp.exp2(stb[rows, :] * SCALE_LOG2 - top)
            dpt = lax.dot_general(kvb[rows, HD:], dx, NT, preferred_element_type=F32)
            dpb[rows, :] = dpt
            stb[rows, :] = weights
            return total + fold(weights, size, jnp.sum), weighted + fold(weights * dpt, size, jnp.sum)

        zero = jnp.zeros((8, ROWS), F32)
        total, weighted = run(last + 1, weigh_step, (zero, zero))
        inverse = 1.0 / jnp.sum(total, axis=0, keepdims=True)
        delta = jnp.sum(weighted, axis=0, keepdims=True) * inverse
        dqt[...] = jnp.zeros((HD, ROWS), F32)

        def grad_step(rows, size, state):
            probs = stb[rows, :] * inverse
            low = probs.astype(BF)
            grads = (probs * (dpb[rows, :] - delta)).astype(BF)
            dv[rows, :] += lax.dot_general(low, dx, NN, preferred_element_type=F32)
            dk[rows, :] += lax.dot_general(grads, qx, NN, preferred_element_type=F32)
            dqt[...] += lax.dot_general(kvb[rows, :HD], grads, TN, preferred_element_type=F32)
            return state

        run(last + 1, grad_step, 0)
        dq = dqt[...].T
        for h in range(4):
            dq_out[x, :, h * HD : (h + 1) * HD] = (dq[h * BLK : (h + 1) * BLK, :] * SCALE).astype(BF)
        return carry

    lax.fori_loop(0, NX, tile, 0)

    def finish(i, carry):
        rows = pl.ds(pl.multiple_of(i * 256, 256), 256)
        dkvb[rows, :HD] = (dk[rows, :] * SCALE).astype(BF)
        dkvb[rows, HD:] = dv[rows, :].astype(BF)
        return carry

    lax.fori_loop(0, 16, finish, 0)

    def store(block, carry):
        pltpu.make_async_copy(dkvb.at[at_place(block), :], dkv_out.at[block], out_sem).start()
        return carry

    lax.fori_loop(0, BLOCKS, store, 0)
    wait_bytes(dkvb, out_sem)


def attention(block_order, qx, dox, kv):
    tokens = BLOCKS * BLK
    return pl.pallas_call(
        attention_kernel,
        name="attention",
        out_shape=(
            jax.ShapeDtypeStruct((NX, BLK, GROUP_COLS), BF),
            jax.ShapeDtypeStruct((BLOCKS, BLK, KV_W), BF),
        ),
        in_specs=[pl.BlockSpec(memory_space=pltpu.SMEM)] + [ANY_SPEC] * 3,
        out_specs=(VMEM_SPEC, ANY_SPEC),
        scratch_shapes=[
            pltpu.VMEM((tokens, KV_W), BF),
            pltpu.VMEM((NX, ROWS, HD), BF),
            pltpu.VMEM((NX, ROWS, HD), BF),
            pltpu.VMEM((tokens, ROWS), F32),
            pltpu.VMEM((tokens, ROWS), F32),
            pltpu.VMEM((tokens, HD), F32),
            pltpu.VMEM((tokens, HD), F32),
            pltpu.VMEM((HD, ROWS), F32),
            pltpu.VMEM((tokens, KV_W), BF),
            DMA,
            DMA,
            DMA,
            DMA,
        ],
        compiler_params=pltpu.CompilerParams(vmem_limit_bytes=56 * 2**20),
        cost_estimate=pl.CostEstimate(flops=10**10, bytes_accessed=8 * 2**20, transcendentals=10**7),
    )(block_order, qx, dox, kv)


class Ring:
    def __init__(self, count, position, neighbour, own, slots, send_sems, recv_sems):
        self.count, self.position, self.neighbour, self.own = count, position, neighbour, own
        self.slots, self.send_sems, self.recv_sems = slots, send_sems, recv_sems
        self.steps = count // 2
        self.sent = []

    def chains(self, step):
        for way in range(2):
            for part in range(2):
                length = self.steps if way == part else self.steps - 1
                if step >= self.steps - length:
                    yield way, part, step == self.steps - length

    def step(self, step):
        for way, part, first in self.chains(step):
            sign = 1 if way == 0 else -1
            target = around(self.position + sign * (self.steps - step), self.count)
            mine = self.own(part, target)
            if first:
                src = mine
            else:
                src = self.slots.at[way, part, step - 1]
                wait_bytes(src, self.recv_sems.at[way, part, step - 1])
                src[...] = (src[...].astype(F32) + mine[...].astype(F32)).astype(BF)
            copy = remote(
                src,
                self.slots.at[way, part, step],
                self.send_sems.at[way, part, step],
                self.recv_sems.at[way, part, step],
                self.neighbour(sign),
            )
            copy.start()
            self.sent.append(copy)

    def result(self, part):
        total = self.own(part, self.position)[...].astype(F32)
        for way in range(2):
            slot = self.slots.at[way, part, self.steps - 1]
            wait_bytes(slot, self.recv_sems.at[way, part, self.steps - 1])
            total += slot[...].astype(F32)
        return total.astype(BF)

    def finish(self):
        for copy in self.sent:
            copy.wait_send()


def rows_at(ref, start, size):
    return ref.at[pl.ds(pl.multiple_of(start, 16), size), :]


def back_kernel(
    dq, dkv, tok, masks, query_grad, key_out, value_out,
    own, other, z1, home_src, raw, tokq, tokt, preall, wa, wb, az, ra, ax, fa, bx, rb, bz, fb, final,
    own_sem, ex_sem, z1_send, z1_recv, home_send, home_recv, tok_send, tok_recv, dq_send, dq_recv,
    pre_send, pre_recv, pfw_send, pfw_recv, core_sem,
    az_send, az_recv, ax_send, ax_recv, bx_send, bx_recv, bz_send, bz_recv, fin_send, fin_recv,
):
    X, Y, Z, C = here()
    head, low = Y // 2, lax.rem(Y, 2)
    unit_core = X // 2
    slot = lax.rem(X, 2)
    same = unit_core == C
    partner = device(X, Y, Z, 1 - C)
    seq = low * 2 + C

    load_own = pltpu.make_async_copy(dkv.at[pl.ds(C * 16, 16)], own, own_sem)
    load_own.start()

    def z_next(sign):
        return device(X, Y, around(Z + sign, NZ), C)

    def x_next(sign):
        return device(around(X + sign, NX), Y, Z, C)

    def y_next(by):
        return device(X, around(Y + by, NY), Z, C)

    ways = (1, 3, 2)
    own_final = jnp.logical_and(
        2 * head + low == X, jnp.where(head == 0, 4 * C + Z // 2 == Z, 4 * C + X == Z)
    )

    signal(partner)
    for xs in range(2):
        for cs in range(NC):
            @pl.when(jnp.logical_not(jnp.logical_and(2 * C + xs == X, C == cs)))
            def _(xs=xs, cs=cs):
                signal(device(2 * C + xs, Y, Z, cs))
    for sign in (1, -1):
        signal(z_next(sign))
        signal(x_next(sign))
    for cs in range(NC):
        signal(device(X, 2 * head + 1 - low, Z, cs))
    for by in ways:
        signal(y_next(by))
    for i in range(8):
        xs = (1 - head) * (i % 4) + head * lax.rem(Z, 4)
        zs = (1 - head) * (2 * lax.rem(Z, 4) + i // 4) + head * i
        ys, cs = X, Z // 4
        is_self = jnp.logical_and(jnp.logical_and(xs == X, zs == Z), jnp.logical_and(ys == Y, cs == C))

        @pl.when(jnp.logical_not(is_self))
        def _(xs=xs, ys=ys, zs=zs, cs=cs):
            signal(device(xs, ys, zs, cs))
    pl.semaphore_wait(
        pltpu.get_barrier_semaphore(), 22 - same.astype(jnp.int32) - own_final.astype(jnp.int32)
    )

    exchange = remote(dkv.at[pl.ds((1 - C) * 16, 16)], other, ex_sem.at[0], ex_sem.at[1], partner)
    exchange.start()
    for xs in range(NX):
        cols = pl.ds(pl.multiple_of((slot * 8 + C * 4) * HD, GROUP_COLS), GROUP_COLS)
        is_self = jnp.logical_and(same, X == xs)
        send_or_copy(
            is_self, dq.at[xs], query_grad.at[0, :, cols], dq_send.at[xs], dq_recv, device(xs, Y, Z, unit_core)
        )
    for quarter in range(4):
        is_self = seq == quarter
        send_or_copy(
            is_self,
            tok.at[0, :, pl.ds(quarter * QUARTER, QUARTER)],
            tokq.at[seq],
            tok_send.at[quarter],
            tok_recv,
            device(X, 2 * head + quarter // 2, Z, quarter % 2),
        )

    load_own.wait()
    exchange.wait_recv()

    def add(i, carry):
        own[i] = (own[i].astype(F32) + other[i].astype(F32)).astype(BF)
        return carry

    lax.fori_loop(0, 16, add, 0)
    ring = Ring(NZ, Z, z_next, lambda part, t: own.at[part * NZ + t], z1, z1_send, z1_recv)
    for step in range(ring.steps):
        ring.step(step)
    for part in range(2):
        home_src[part] = ring.result(part)
        xs = 2 * C + part
        is_self = jnp.logical_and(same, X == xs)
        send_or_copy(
            is_self,
            home_src.at[part],
            raw.at[slot],
            home_send.at[part],
            home_recv,
            device(xs, Y, Z, unit_core),
        )
    wait_bytes(tokq, tok_recv)
    for s in range(4):
        tokt[:, s * BLK : (s + 1) * BLK] = tokq[s].T

    wait_bytes(raw, home_recv)
    my_rows = pl.ds(pl.multiple_of(seq * BLK, BLK), BLK)
    for j in range(2):
        for what in range(2):
            mask = masks[what, 0, :, j * HD : (j + 1) * HD] != 0
            piece = raw[j, :, what * HD : (what + 1) * HD]
            first = (2 * j + what) * HD
            preall[head, my_rows, first : first + HD] = jnp.where(mask, piece, jnp.zeros_like(piece))
    mine = preall.at[head, my_rows, :]
    sends = [
        remote(mine, mine, pre_send.at[i], pre_recv.at[i], y_next(by)) for i, by in enumerate(ways)
    ] + [remote(mine, mine, core_sem.at[0], core_sem.at[1], partner)]
    for copy in sends:
        copy.start()

    def piece_of(by, core):
        ys = around(Y + NY - by, NY)
        start = (lax.rem(ys, 2) * 2 + core) * BLK
        return preall.at[ys // 2, pl.ds(pl.multiple_of(start, BLK), BLK), :]

    forwards = []
    for i, by in enumerate(ways):
        piece = piece_of(by, C)
        wait_bytes(piece, pre_recv.at[i])
        copy = remote(piece, piece, pfw_send.at[i], pfw_recv.at[i], partner)
        copy.start()
        forwards.append(copy)
    sends[3].wait_recv()
    for copy in forwards:
        copy.wait_recv()

    for which, out in ((0, wa), (1, wb)):
        def multiply(i, carry, which=which, out=out):
            rows = pl.ds(pl.multiple_of(i * 256, 256), 256)
            out[rows, :] = jnp.dot(tokt[rows, :], preall[which], preferred_element_type=F32).astype(BF)
            return carry

        lax.fori_loop(0, 4, multiply, 0)

    a_first = Ring(NZ, Z, z_next, lambda part, t: rows_at(wa, t * 128 + part * 64, 64), az, az_send, az_recv)
    b_first = Ring(NX, X, x_next, lambda part, t: rows_at(wb, t * 256 + part * 128, 128), bx, bx_send, bx_recv)
    a_next = Ring(NX, X, x_next, lambda part, t: rows_at(ra, t * 32 + part * 16, 16), ax, ax_send, ax_recv)
    b_next = Ring(NZ, Z, z_next, lambda part, t: rows_at(rb, t * 32 + part * 16, 16), bz, bz_send, bz_recv)
    a_first.step(0)
    b_first.step(0)
    a_first.step(1)
    b_first.step(1)
    a_first.step(2)
    for part in range(2):
        rb[part * 128 : (part + 1) * 128, :] = b_first.result(part)
    b_next.step(0)
    a_first.step(3)
    b_next.step(1)
    for part in range(2):
        ra[part * 64 : (part + 1) * 64, :] = a_first.result(part)
    a_next.step(0)
    b_next.step(2)
    a_next.step(1)
    b_next.step(3)
    for part in range(2):
        fa[part * 16 : (part + 1) * 16, :] = a_next.result(part)
    for part in range(2):
        fb[part * 16 : (part + 1) * 16, :] = b_next.result(part)

    a_rows = rows_at(final, lax.rem(Z, 2) * 128 + X * 32, 32)
    b_rows = rows_at(final, Z * 32, 32)
    final_sends = []
    for which, src, dst, zs in ((0, fa, a_rows, 4 * C + Z // 2), (1, fb, b_rows, 4 * C + X)):
        for low2 in range(2):
            for c2 in range(NC):
                target = device(2 * head + low, 2 * which + low2, zs, c2)
                is_self = jnp.logical_and(
                    own_final, jnp.logical_and(head == which, jnp.logical_and(low == low2, C == c2))
                )
                sem = fin_send.at[which, low2, c2]
                send_or_copy(is_self, src, dst, sem, fin_recv, target)
                final_sends.append((is_self, src, sem))
    wait_bytes(final, fin_recv)
    for j in range(2):
        for what, out in ((0, key_out), (1, value_out)):
            first = (2 * j + what) * HD
            out[:, j * HD : (j + 1) * HD] = final[:, first : first + HD].astype(F32) * 0.25

    wait_bytes(query_grad, dq_recv)
    exchange.wait_send()
    for xs in range(NX):
        wait_sent(jnp.logical_and(same, X == xs), dq.at[xs], dq_send.at[xs])
    for quarter in range(4):
        wait_sent(seq == quarter, tokq.at[0], tok_send.at[quarter])
    for part in range(2):
        wait_sent(jnp.logical_and(same, X == 2 * C + part), raw.at[part], home_send.at[part])
    for copy in sends + forwards:
        copy.wait_send()
    for each in (ring, a_first, b_first, a_next, b_next):
        each.finish()
    for is_self, src, sem in final_sends:
        wait_sent(is_self, src, sem)


def back(dq, dkv, tokens, clip_masks):
    def slots(steps, rows, cols):
        return pltpu.VMEM((2, 2, steps, rows, cols), BF)

    wide = 2 * KV_W
    return pl.pallas_call(
        back_kernel,
        name="back",
        out_shape=(
            jax.ShapeDtypeStruct((1, BLK, 2048), BF),
            jax.ShapeDtypeStruct((256, KV_W), F32),
            jax.ShapeDtypeStruct((256, KV_W), F32),
        ),
        in_specs=[ANY_SPEC] * 3 + [VMEM_SPEC],
        out_specs=(ANY_SPEC, VMEM_SPEC, VMEM_SPEC),
        scratch_shapes=[
            pltpu.VMEM((16, BLK, KV_W), BF),
            pltpu.VMEM((16, BLK, KV_W), BF),
            slots(4, BLK, KV_W),
            pltpu.VMEM((2, BLK, KV_W), BF),
            pltpu.VMEM((2, BLK, KV_W), BF),
            pltpu.VMEM((4, BLK, QUARTER), BF),
            pltpu.VMEM((QUARTER, 4 * BLK), BF),
            pltpu.VMEM((2, 4 * BLK, wide), BF),
            pltpu.VMEM((QUARTER, wide), BF),
            pltpu.VMEM((QUARTER, wide), BF),
            slots(4, 64, wide),
            pltpu.VMEM((128, wide), BF),
            slots(2, 16, wide),
            pltpu.VMEM((32, wide), BF),
            slots(2, 128, wide),
            pltpu.VMEM((256, wide), BF),
            slots(4, 16, wide),
            pltpu.VMEM((32, wide), BF),
            pltpu.VMEM((256, wide), BF),
            DMA,
            DMA((2,)),
            DMA((2, 2, 4)),
            DMA((2, 2, 4)),
            DMA((2,)),
            DMA,
            DMA((4,)),
            DMA,
            DMA((4,)),
            DMA,
            DMA((3,)),
            DMA((3,)),
            DMA((3,)),
            DMA((3,)),
            DMA((2,)),
            DMA((2, 2, 4)),
            DMA((2, 2, 4)),
            DMA((2, 2, 2)),
            DMA((2, 2, 2)),
            DMA((2, 2, 2)),
            DMA((2, 2, 2)),
            DMA((2, 2, 4)),
            DMA((2, 2, 4)),
            DMA((2, 2, 2)),
            DMA,
        ],
        compiler_params=pltpu.CompilerParams(
            collective_id=1, has_side_effects=True, vmem_limit_bytes=40 * 2**20
        ),
        cost_estimate=pl.CostEstimate(flops=10**9, bytes_accessed=16 * 2**20, transcendentals=0),
    )(dq, dkv, tokens, clip_masks)


def on_device(
    tokens, queries, out_grad, key_weight, value_weight, noise_codes, clip_masks, block_order
):
    qx, dox, kv = front(tokens, queries, out_grad, key_weight, value_weight, noise_codes)
    dq, dkv = attention(block_order, qx, dox, kv)
    return back(dq, dkv, tokens, clip_masks)


def solution(mesh):
    placed = (
        P("dp", "ctx", "head"),
        P("dp", "ctx", "head"),
        P("dp", "ctx", "head"),
        P(None, "head"),
        P(None, "head"),
        P(None, "dp", "ctx", "head"),
        P(None, "dp", "ctx", "head"),
        P(),
    )
    return jax.shard_map(
        on_device,
        mesh=mesh,
        in_specs=placed,
        out_specs=(P("dp", "ctx", "head"), P("ctx", "head"), P("ctx", "head")),
        check_vma=False,
    )
```

time: 1130 us -> 176 us (0.16)
  waiting for transfers between devices: 568 us -> 0 us
  starting transfers between devices: 188 us -> 0 us
  Pallas kernels: 0 us -> 157 us
  other arithmetic: 118 us -> 0 us
  loops' own time: 110 us -> 0 us
  matrix products: 55.5 us -> 0 us
  local copies, waits for them, and re-layouts: 70.4 us -> 16.4 us
  between operations: 14.5 us -> 0.71 us
    reduce_scatter x1 -> x0, waiting for transfers between devices: 283 us -> none  [on_device(): lax.psum_scatter(lax.dot_general(whole_x, flat_grads, contract, preferred...]
    ppermute x32 -> x0, starting transfers between devices: 188 us -> none  [from_behind(): lax.ppermute(array, axis, [(i, (i + by) % count) for i in range(count)])]
    pallas_call x0 -> x3, Pallas kernels: none -> 157 us  [the longest x1 87.6 us: back(): pl.pallas_call(back_kernel, name='back', out_shape=(jax.ShapeDtypeStruct(...]
    ppermute x32 -> x0, waiting for transfers between devices: 122 us -> none  [from_behind(): lax.ppermute(array, axis, [(i, (i + by) % count) for i in range(count)])]
    all_gather x2 -> x0, waiting for transfers between devices: 116 us -> none  [the longest x1 71.8 us: on_device(): all_kv = lax.all_gather(local_kv, 'ctx', axis=0, tiled=True)]
    another operation x66 -> x0, loops' own time: 110 us -> none  [the longest x1 43.3 us: on_device(): lax.fori_loop(0, cycle_size, cycle_step, (zero_query, zero_pair))]
    add x118 -> x0, other arithmetic: 65.4 us -> none  [the longest x32 53.9 us: cycle_step(): travel = from_behind(travel + pair_add, 'ctx', 1)]
    dot_general x129 -> x0, matrix products: 55.5 us -> none  [the longest x36 14 us: block_scores(): jnp.einsum('qjgd,kjd->jgqk', query_heads, key_block, preferred_element_ty...]
  transfers between devices with their start and end apart: 36 -> 0, of which waited for: 36 -> 0; matrix products, arithmetic and copies ran while one was open for 1% -> 0% of each run, Pallas kernels for 0% -> 0%
where the time goes in v1:
time: 176 us; the launch traced here: 174 us
  Pallas kernels  157 us (89%)
  local copies, waits for them, and re-layouts  16.4 us (9%)
    pallas_call x1, Pallas kernels, back(): pl.pallas_call(back_kernel, name='back', out_shape=(jax.ShapeDtypeStruct(...  87.6 us
    pallas_call x1, Pallas kernels, front(): pl.pallas_call(front_kernel, name='front', out_shape=(jax.ShapeDtypeStruc...  45.3 us
    pallas_call x1, Pallas kernels, attention(): pl.pallas_call(attention_kernel, name='attention', out_shape=(jax.ShapeDt...  24.3 us
    unnamed x29, local copies, waits for them, and re-layouts  16.4 us

profile of v1, /device:TPU:71, one launch (start us, length us, event | category | flops | bytes accessed | tf_op | source)
XLA Modules:
  0.0 174.3 jit_solution(9335563568202640135)
XLA Ops:
  0.6 0.0 copy-start
  0.6 2.2 %copy-done = bf16[8192,256]{1,0:T(8,128)(2,1)S(1)} copy-done((bf16[8192,256]{1,0:T(8,128)(2,1)S(1)}, bf16[8192,256]{1,0:T(8,128)(2,1)}, u32[]{:S(2)}) %copy-start) | copy-done | bytes 4194328
  2.8 0.0 copy-start.1
  2.8 2.2 %copy-done.1 = bf16[8192,256]{1,0:T(8,128)(2,1)S(1)} copy-done((bf16[8192,256]{1,0:T(8,128)(2,1)S(1)}, bf16[8192,256]{1,0:T(8,128)(2,1)}, u32[]{:S(2)}) %copy-start.1) | copy-done | bytes 4194328
  5.0 0.0 copy-start.2
  5.0 1.2 copy-done.2
  6.2 0.0 copy-start.6
  6.2 1.0 copy-done.6
  7.3 0.0 copy-start.7
  7.3 1.0 copy-done.7
  8.3 0.0 copy-start.9
  8.3 0.9 copy-done.9
  9.3 45.3 %front.1 = (bf16[4,128,512]{2,1,0:T(8,128)(2,1)S(1)}, bf16[4,128,512]{2,1,0:T(8,128)(2,1)S(1)}, bf16[32,128,256]{2,1,0:T(8,128)(2,1)S(1)}) custom-call(bf16[1,128,4096]{2,1,0:T(8,128)(2,1)S(1)} %copy-done.2, bf16[1,128,2048]{2,1,0:T(8,128)(2,1)S(1)} %copy-done.6, bf16[1,128,2048]{2,1,0:T(8,128)(2,1)S(1)} %copy-done.7, bf16[8192,256]{1,0:T(8,128)(2,1)S(1)} %copy-done, ...), custom_call_target="tpu_custom_call" | custom-call | flops 1000000000 | bytes 16777216 | tf_op jit(solution)/shard_map/front/pallas_call | solution.py:195
  54.6 0.0 copy-start.10
  54.6 1.3 copy-done.10
  55.9 0.0 copy-start.11
  55.9 0.8 copy-done.11
  56.7 0.0 copy-start.12
  56.7 0.8 copy-done.12
  57.5 0.0 copy-start.3
  57.5 0.0 copy-start.8
  57.5 24.3 %attention.1 = (bf16[4,128,512]{2,1,0:T(8,128)(2,1)}, bf16[32,128,256]{2,1,0:T(8,128)(2,1)}) custom-call(s32[32]{0:T(128)} %order.1, bf16[4,128,512]{2,1,0:T(8,128)(2,1)} %copy-done.11, bf16[4,128,512]{2,1,0:T(8,128)(2,1)} %copy-done.12, bf16[32,128,256]{2,1,0:T(8,128)(2,1)} %copy-done.10), custom_call_target="tpu_custom_call" | custom-call | flops 10000000000 | bytes 8388608 | tf_op jit(solution)/shard_map/attention/pallas_call | solution.py:352
  81.8 0.0 copy-done.3
  81.8 0.0 copy-done.8
  81.8 0.0 copy-start.4
  81.8 1.6 copy-done.4
  83.4 0.0 copy-start.5
  83.4 1.0 copy-done.5
  84.4 87.6 %back.1 = (bf16[1,128,2048]{2,1,0:T(8,128)(2,1)S(1)}, f32[256,256]{1,0:T(8,128)S(1)}, f32[256,256]{1,0:T(8,128)S(1)}) custom-call(bf16[4,128,512]{2,1,0:T(8,128)(2,1)S(1)} %copy-done.5, bf16[32,128,256]{2,1,0:T(8,128)(2,1)S(1)} %copy-done.4, bf16[1,128,4096]{2,1,0:T(8,128)(2,1)S(1)} %copy-done.3, s32[2,1,128,256]{3,2,1,0:T(8,128)S(1)} %copy-done.8), custom_call_target="tpu_custom_call" | custom-call | flops 1000000000 | bytes 16777216 | tf_op jit(solution)/shard_map/back/pallas_call | solution.py:641
  172.1 0.8 copy.14
  172.9 0.7 copy.15
  173.6 0.7 copy.16
Async XLA Ops:
  0.6 2.2 %copy-start = (bf16[8192,256]{1,0:T(8,128)(2,1)S(1)}, bf16[8192,256]{1,0:T(8,128)(2,1)}, u32[]{:S(2)}) copy-start(bf16[8192,256]{1,0:T(8,128)(2,1)} %kw.1) | copy-start | bytes 12582916
  2.8 2.2 %copy-start.1 = (bf16[8192,256]{1,0:T(8,128)(2,1)S(1)}, bf16[8192,256]{1,0:T(8,128)(2,1)}, u32[]{:S(2)}) copy-start(bf16[8192,256]{1,0:T(8,128)(2,1)} %vw.1) | copy-start | bytes 12582916
  5.0 1.2 copy-start.2
  6.2 1.0 copy-start.6
  7.3 1.0 copy-start.7
  8.3 0.9 copy-start.9
  54.6 1.3 copy-start.10
  55.9 0.8 copy-start.11
  56.7 0.8 copy-start.12
  57.5 24.3 %copy-start.3 = (bf16[1,128,4096]{2,1,0:T(8,128)(2,1)S(1)}, bf16[1,128,4096]{2,1,0:T(8,128)(2,1)}, u32[]{:S(2)}) copy-start(bf16[1,128,4096]{2,1,0:T(8,128)(2,1)} %tok.3) | copy-start | bytes 3145732
  57.5 24.3 %copy-start.8 = (s32[2,1,128,256]{3,2,1,0:T(8,128)S(1)}, s32[2,1,128,256]{3,2,1,0:T(8,128)}, u32[]{:S(2)}) copy-start(s32[2,1,128,256]{3,2,1,0:T(8,128)} %masks.1) | copy-start | bytes 786436
  81.8 1.6 copy-start.4
  83.4 1.0 copy-start.5

commit v2 on v1

--- a/solution.py
+++ b/solution.py
@@ -24,6 +24,7 @@
 BF = jnp.bfloat16
 F32 = jnp.float32
 MESH = pl.DeviceIdType.MESH
+VMEM_GRANT = 62 * 2**20
 NT = (((1,), (1,)), ((), ()))
 NN = (((1,), (0,)), ((), ()))
 TN = (((0,), (0,)), ((), ()))
@@ -77,9 +78,9 @@
 
 
 def front_kernel(
-    tok, q, do, kw, vw, codes, qx, dox, kv,
-    xbuf, wbuf, acc, kvst,
-    w_sem, own_sem, tok_send, tok_recv, q_send, q_recv, kv_send, kv_send0, kv_recv, fw_send, fw_recv,
+    tok, q, do, kw, vw, codes_in, qx, dox, kv,
+    codes, xbuf, wbuf, acc, kvst,
+    codes_sem, w_sem, own_sem, tok_send, tok_recv, q_send, q_recv, kv_send, kv_send0, kv_recv, fw_send, fw_recv,
 ):
     X, Y, Z, C = here()
     head = Y // 2
@@ -88,7 +89,7 @@
     peer = device(X, around(Y + 2, NY), Z, C)
     partner = device(X, Y, Z, 1 - C)
 
-    loads = []
+    loads = [pltpu.make_async_copy(codes_in, codes, codes_sem)]
     for half in range(2):
         rows = pl.ds(half * HALF_D, HALF_D)
         loads.append(pltpu.make_async_copy(kw.at[rows, :], wbuf.at[half, :, pl.ds(0, KV_W)], w_sem.at[half, 0]))
@@ -200,13 +201,15 @@
             jax.ShapeDtypeStruct((NX, BLK, GROUP_COLS), BF),
             jax.ShapeDtypeStruct((BLOCKS, BLK, KV_W), BF),
         ),
-        in_specs=[ANY_SPEC] * 5 + [VMEM_SPEC],
+        in_specs=[ANY_SPEC] * 6,
         out_specs=(ANY_SPEC,) * 3,
         scratch_shapes=[
+            pltpu.VMEM((2, 1, BLK, KV_W), jnp.int32),
             pltpu.VMEM((2, BLK, HALF_D), BF),
             pltpu.VMEM((2, HALF_D, 2 * KV_W), BF),
             pltpu.VMEM((BLK, 2 * KV_W), F32),
             pltpu.VMEM((2, BLK, KV_W), BF),
+            DMA,
             DMA((2, 2)),
             DMA,
             DMA((ROW_CHUNKS,)),
@@ -220,7 +223,7 @@
             DMA((ROW_CHUNKS,)),
         ],
         compiler_params=pltpu.CompilerParams(
-            collective_id=0, has_side_effects=True, vmem_limit_bytes=40 * 2**20
+            collective_id=0, has_side_effects=True, vmem_limit_bytes=VMEM_GRANT
         ),
         cost_estimate=pl.CostEstimate(flops=10**9, bytes_accessed=16 * 2**20, transcendentals=0),
     )(tokens, queries, out_grad, key_weight, value_weight, noise_codes)
@@ -340,7 +343,8 @@
     lax.fori_loop(0, 16, finish, 0)
 
     def store(block, carry):
-        pltpu.make_async_copy(dkvb.at[at_place(block), :], dkv_out.at[block], out_sem).start()
+        dst = dkv_out.at[block // NZ, lax.rem(block, NZ)]
+        pltpu.make_async_copy(dkvb.at[at_place(block), :], dst, out_sem).start()
         return carry
 
     lax.fori_loop(0, BLOCKS, store, 0)
@@ -354,7 +358,7 @@
         name="attention",
         out_shape=(
             jax.ShapeDtypeStruct((NX, BLK, GROUP_COLS), BF),
-            jax.ShapeDtypeStruct((BLOCKS, BLK, KV_W), BF),
+            jax.ShapeDtypeStruct((NX, NZ, BLK, KV_W), BF),
         ),
         in_specs=[pl.BlockSpec(memory_space=pltpu.SMEM)] + [ANY_SPEC] * 3,
         out_specs=(VMEM_SPEC, ANY_SPEC),
@@ -373,7 +377,7 @@
             DMA,
             DMA,
         ],
-        compiler_params=pltpu.CompilerParams(vmem_limit_bytes=56 * 2**20),
+        compiler_params=pltpu.CompilerParams(vmem_limit_bytes=VMEM_GRANT),
         cost_estimate=pl.CostEstimate(flops=10**10, bytes_accessed=8 * 2**20, transcendentals=10**7),
     )(block_order, qx, dox, kv)
 
@@ -395,8 +399,7 @@
     def step(self, step):
         for way, part, first in self.chains(step):
             sign = 1 if way == 0 else -1
-            target = around(self.position + sign * (self.steps - step), self.count)
-            mine = self.own(part, target)
+            mine = self.own(part, sign * (self.steps - step))
             if first:
                 src = mine
             else:
@@ -414,7 +417,7 @@
             self.sent.append(copy)
 
     def result(self, part):
-        total = self.own(part, self.position)[...].astype(F32)
+        total = self.own(part, 0)[...].astype(F32)
         for way in range(2):
             slot = self.slots.at[way, part, self.steps - 1]
             wait_bytes(slot, self.recv_sems.at[way, part, self.steps - 1])
@@ -426,16 +429,21 @@
             copy.wait_send()
 
 
-def rows_at(ref, start, size):
-    return ref.at[pl.ds(pl.multiple_of(start, 16), size), :]
+def span(start, size):
+    return pl.ds(pl.multiple_of(start, 16), size)
+
+
+HALF_ROWS = BLK // 2
+DELTAS = (4, 3, -3, 2, -2, 1, -1, 0)
 
 
 def back_kernel(
     dq, dkv, tok, masks, query_grad, key_out, value_out,
-    own, other, z1, home_src, raw, tokq, tokt, preall, wa, wb, az, ra, ax, fa, bx, rb, bz, fb, final,
-    own_sem, ex_sem, z1_send, z1_recv, home_send, home_recv, tok_send, tok_recv, dq_send, dq_recv,
+    own, other, z1, home_src, raw, mbuf, tokq, tokt, preall, wa, wb, az, ra, ax, fa, bx, rb, bz, fb, final,
+    own_sem, mask_sem, ex_send, ex_recv, z1_send, z1_recv, home_send, home_recv, tok_send, tok_recv, dq_send, dq_recv,
     pre_send, pre_recv, pfw_send, pfw_recv, core_sem,
-    az_send, az_recv, ax_send, ax_recv, bx_send, bx_recv, bz_send, bz_recv, fin_send, fin_recv,
+    az_send, az_recv, ax_send, ax_recv, bx_send, bx_recv, bz_send, bz_recv,
+    fin_send, fin_recv, f2_send, f2_recv,
 ):
     X, Y, Z, C = here()
     head, low = Y // 2, lax.rem(Y, 2)
@@ -443,10 +451,13 @@
     slot = lax.rem(X, 2)
     same = unit_core == C
     partner = device(X, Y, Z, 1 - C)
+    beside = device(X, 2 * head + 1 - low, Z, C)
     seq = low * 2 + C
 
-    load_own = pltpu.make_async_copy(dkv.at[pl.ds(C * 16, 16)], own, own_sem)
+    load_own = pltpu.make_async_copy(dkv.at[pl.ds(C * 2, 2)], own, own_sem)
     load_own.start()
+    load_mask = pltpu.make_async_copy(masks, mbuf, mask_sem)
+    load_mask.start()
 
     def z_next(sign):
         return device(X, Y, around(Z + sign, NZ), C)
@@ -458,9 +469,16 @@
         return device(X, around(Y + by, NY), Z, C)
 
     ways = (1, 3, 2)
-    own_final = jnp.logical_and(
-        2 * head + low == X, jnp.where(head == 0, 4 * C + Z // 2 == Z, 4 * C + X == Z)
-    )
+    i_mine = X + 4 * lax.rem(Z, 2)
+    member = i_mine // 2
+    target_a = (Y, member // 2, 4 * C + Z // 2, lax.rem(member, 2))
+    target_b = (Y, 2 + member // 2, 4 * C + Z // 2, lax.rem(member, 2))
+
+    def is_me(place):
+        x, y, z, core = place
+        return jnp.logical_and(jnp.logical_and(x == X, y == Y), jnp.logical_and(z == Z, core == C))
+
+    self_a, self_b = is_me(target_a), is_me(target_b)
 
     signal(partner)
     for xs in range(2):
@@ -475,21 +493,15 @@
         signal(device(X, 2 * head + 1 - low, Z, cs))
     for by in ways:
         signal(y_next(by))
-    for i in range(8):
-        xs = (1 - head) * (i % 4) + head * lax.rem(Z, 4)
-        zs = (1 - head) * (2 * lax.rem(Z, 4) + i // 4) + head * i
-        ys, cs = X, Z // 4
-        is_self = jnp.logical_and(jnp.logical_and(xs == X, zs == Z), jnp.logical_and(ys == Y, cs == C))
-
-        @pl.when(jnp.logical_not(is_self))
-        def _(xs=xs, ys=ys, zs=zs, cs=cs):
-            signal(device(xs, ys, zs, cs))
-    pl.semaphore_wait(
-        pltpu.get_barrier_semaphore(), 22 - same.astype(jnp.int32) - own_final.astype(jnp.int32)
-    )
-
-    exchange = remote(dkv.at[pl.ds((1 - C) * 16, 16)], other, ex_sem.at[0], ex_sem.at[1], partner)
-    exchange.start()
+    signal(device(around(X + 2, NX), Y, Z, C))
+    pl.semaphore_wait(pltpu.get_barrier_semaphore(), 15 - same.astype(jnp.int32))
+
+    exchanges = {}
+    for i, delta in enumerate(DELTAS):
+        t = around(Z + delta, NZ)
+        copy = remote(dkv.at[pl.ds((1 - C) * 2, 2), t], other.at[:, t], ex_send.at[i], ex_recv.at[i], partner)
+        copy.start()
+        exchanges[delta] = copy
     for xs in range(NX):
         cols = pl.ds(pl.multiple_of((slot * 8 + C * 4) * HD, GROUP_COLS), GROUP_COLS)
         is_self = jnp.logical_and(same, X == xs)
@@ -508,135 +520,216 @@
         )
 
     load_own.wait()
-    exchange.wait_recv()
-
-    def add(i, carry):
-        own[i] = (own[i].astype(F32) + other[i].astype(F32)).astype(BF)
-        return carry
-
-    lax.fori_loop(0, 16, add, 0)
-    ring = Ring(NZ, Z, z_next, lambda part, t: own.at[part * NZ + t], z1, z1_send, z1_recv)
-    for step in range(ring.steps):
-        ring.step(step)
-    for part in range(2):
-        home_src[part] = ring.result(part)
-        xs = 2 * C + part
-        is_self = jnp.logical_and(same, X == xs)
-        send_or_copy(
-            is_self,
-            home_src.at[part],
-            raw.at[slot],
-            home_send.at[part],
-            home_recv,
-            device(xs, Y, Z, unit_core),
-        )
+    ready = set()
+
+    def prepare(delta):
+        if delta in ready:
+            return
+        ready.add(delta)
+        t = around(Z + delta, NZ)
+        exchanges[delta].wait_recv()
+        for part in range(2):
+            own[part, t] = (own[part, t].astype(F32) + other[part, t].astype(F32)).astype(BF)
+
+    def own_part(half):
+        def get(part, delta):
+            prepare(4 if delta == -4 else delta)
+            return own.at[part, around(Z + delta, NZ), pl.ds(half * HALF_ROWS, HALF_ROWS), :]
+
+        return get
+
+    rings = [
+        Ring(NZ, Z, z_next, own_part(half), z1.at[half], z1_send.at[half], z1_recv.at[half]) for half in range(2)
+    ]
+    for step in range(NZ // 2):
+        for ring in rings:
+            ring.step(step)
+    for half, ring in enumerate(rings):
+        rows = pl.ds(half * HALF_ROWS, HALF_ROWS)
+        for part in range(2):
+            home_src[part, rows, :] = ring.result(part)
+            xs = 2 * C + part
+            is_self = jnp.logical_and(same, X == xs)
+            send_or_copy(
+                is_self,
+                home_src.at[part, rows, :],
+                raw.at[slot, rows, :],
+                home_send.at[half, part],
+                home_recv.at[half],
+                device(xs, Y, Z, unit_core),
+            )
+
+    load_mask.wait()
+    sends = []
+
+    def my_rows(half):
+        return span(seq * BLK + half * HALF_ROWS, HALF_ROWS)
+
+    for half in range(2):
+        rows = pl.ds(half * HALF_ROWS, HALF_ROWS)
+        wait_bytes(raw.at[:, rows, :], home_recv.at[half])
+        for j in range(2):
+            for what in range(2):
+                mask = mbuf[what, 0, rows, j * HD : (j + 1) * HD] != 0
+                piece = raw[j, rows, what * HD : (what + 1) * HD]
+                first = (2 * j + what) * HD
+                preall[head, my_rows(half), first : first + HD] = jnp.where(mask, piece, jnp.zeros_like(piece))
+        mine = preall.at[head, my_rows(half), :]
+        for i, by in enumerate(ways):
+            sends.append(remote(mine, mine, pre_send.at[half, i], pre_recv.at[half, i], y_next(by)))
+            sends[-1].start()
+        sends.append(remote(mine, mine, core_sem.at[half, 0], core_sem.at[half, 1], partner))
+        sends[-1].start()
+
     wait_bytes(tokq, tok_recv)
     for s in range(4):
-        tokt[:, s * BLK : (s + 1) * BLK] = tokq[s].T
-
-    wait_bytes(raw, home_recv)
-    my_rows = pl.ds(pl.multiple_of(seq * BLK, BLK), BLK)
-    for j in range(2):
-        for what in range(2):
-            mask = masks[what, 0, :, j * HD : (j + 1) * HD] != 0
-            piece = raw[j, :, what * HD : (what + 1) * HD]
-            first = (2 * j + what) * HD
-            preall[head, my_rows, first : first + HD] = jnp.where(mask, piece, jnp.zeros_like(piece))
-    mine = preall.at[head, my_rows, :]
-    sends = [
-        remote(mine, mine, pre_send.at[i], pre_recv.at[i], y_next(by)) for i, by in enumerate(ways)
-    ] + [remote(mine, mine, core_sem.at[0], core_sem.at[1], partner)]
-    for copy in sends:
-        copy.start()
-
-    def piece_of(by, core):
-        ys = around(Y + NY - by, NY)
-        start = (lax.rem(ys, 2) * 2 + core) * BLK
-        return preall.at[ys // 2, pl.ds(pl.multiple_of(start, BLK), BLK), :]
+        tokt[:, :, :, s * BLK : (s + 1) * BLK] = tokq[s].T.reshape(NZ, NX, 32, BLK)
 
     forwards = []
-    for i, by in enumerate(ways):
-        piece = piece_of(by, C)
-        wait_bytes(piece, pre_recv.at[i])
-        copy = remote(piece, piece, pfw_send.at[i], pfw_recv.at[i], partner)
-        copy.start()
-        forwards.append(copy)
-    sends[3].wait_recv()
+    for half in range(2):
+        for i, by in enumerate(ways):
+            ys = around(Y + NY - by, NY)
+            start = (lax.rem(ys, 2) * 2 + C) * BLK + half * HALF_ROWS
+            piece = preall.at[ys // 2, span(start, HALF_ROWS), :]
+            wait_bytes(piece, pre_recv.at[half, i])
+            copy = remote(piece, piece, pfw_send.at[half, i], pfw_recv.at[half, i], partner)
+            copy.start()
+            forwards.append(copy)
+    for half in range(2):
+        sends[half * 4 + 3].wait_recv()
     for copy in forwards:
         copy.wait_recv()
 
-    for which, out in ((0, wa), (1, wb)):
-        def multiply(i, carry, which=which, out=out):
-            rows = pl.ds(pl.multiple_of(i * 256, 256), 256)
-            out[rows, :] = jnp.dot(tokt[rows, :], preall[which], preferred_element_type=F32).astype(BF)
-            return carry
-
-        lax.fori_loop(0, 4, multiply, 0)
-
-    a_first = Ring(NZ, Z, z_next, lambda part, t: rows_at(wa, t * 128 + part * 64, 64), az, az_send, az_recv)
-    b_first = Ring(NX, X, x_next, lambda part, t: rows_at(wb, t * 256 + part * 128, 128), bx, bx_send, bx_recv)
-    a_next = Ring(NX, X, x_next, lambda part, t: rows_at(ra, t * 32 + part * 16, 16), ax, ax_send, ax_recv)
-    b_next = Ring(NZ, Z, z_next, lambda part, t: rows_at(rb, t * 32 + part * 16, 16), bz, bz_send, bz_recv)
-    a_first.step(0)
-    b_first.step(0)
-    a_first.step(1)
-    b_first.step(1)
-    a_first.step(2)
-    for part in range(2):
-        rb[part * 128 : (part + 1) * 128, :] = b_first.result(part)
-    b_next.step(0)
-    a_first.step(3)
-    b_next.step(1)
-    for part in range(2):
-        ra[part * 64 : (part + 1) * 64, :] = a_first.result(part)
-    a_next.step(0)
-    b_next.step(2)
-    a_next.step(1)
-    b_next.step(3)
-    for part in range(2):
-        fa[part * 16 : (part + 1) * 16, :] = a_next.result(part)
-    for part in range(2):
-        fb[part * 16 : (part + 1) * 16, :] = b_next.result(part)
-
-    a_rows = rows_at(final, lax.rem(Z, 2) * 128 + X * 32, 32)
-    b_rows = rows_at(final, Z * 32, 32)
-    final_sends = []
-    for which, src, dst, zs in ((0, fa, a_rows, 4 * C + Z // 2), (1, fb, b_rows, 4 * C + X)):
-        for low2 in range(2):
-            for c2 in range(NC):
-                target = device(2 * head + low, 2 * which + low2, zs, c2)
-                is_self = jnp.logical_and(
-                    own_final, jnp.logical_and(head == which, jnp.logical_and(low == low2, C == c2))
-                )
-                sem = fin_send.at[which, low2, c2]
-                send_or_copy(is_self, src, dst, sem, fin_recv, target)
-                final_sends.append((is_self, src, sem))
-    wait_bytes(final, fin_recv)
+    made = set()
+
+    def product(which, delta):
+        if (which, delta) in made:
+            return
+        made.add((which, delta))
+        if which == 0:
+            t = around(Z + delta, NZ)
+            rows = tokt[t].reshape(128, 4 * BLK)
+        else:
+            t = around(X + delta, NX)
+            rows = tokt[:, t].reshape(256, 4 * BLK)
+        value = jnp.dot(rows, preall[which], preferred_element_type=F32).astype(BF)
+        for side in range(2):
+            half = value[:, side * KV_W : (side + 1) * KV_W]
+            if which == 0:
+                wa[side, t] = half.reshape(NX, 32, KV_W)
+            else:
+                wb[side, :, t] = half.reshape(NZ, 32, KV_W)
+
+    def a_own(side):
+        def get(part, delta):
+            delta = 4 if delta == -4 else delta
+            product(0, delta)
+            return wa.at[side, around(Z + delta, NZ), pl.ds(part * 2, 2)]
+
+        return get
+
+    def b_own(side):
+        def get(part, delta):
+            delta = 2 if delta == -2 else delta
+            product(1, delta)
+            return wb.at[side, pl.ds(part * 4, 4), around(X + delta, NX)]
+
+        return get
+
+    a1 = [Ring(NZ, Z, z_next, a_own(s), az.at[s], az_send.at[s], az_recv.at[s]) for s in range(2)]
+    b1 = [Ring(NX, X, x_next, b_own(s), bx.at[s], bx_send.at[s], bx_recv.at[s]) for s in range(2)]
+
+    def go(rings, step):
+        for ring in rings:
+            ring.step(step)
+
+    directs = []
+
+    def direct(source, slots, send_sems, recv_sems, count, position, neighbour):
+        deltas = sorted([d for d in range(1 - count // 2, count // 2 + 1) if d], key=lambda d: -abs(d))
+        for delta in deltas:
+            i = delta % count - 1
+            src = source.at[around(position + delta, count)]
+            copy = remote(src, slots.at[i], send_sems.at[i], recv_sems.at[i], neighbour(delta))
+            copy.start()
+            directs.append(copy)
+
+    def collect(source, slots, recv_sems, count, position):
+        total = source[position].astype(F32)
+        for i in range(count - 1):
+            wait_bytes(slots.at[i], recv_sems.at[i])
+            total += slots[i].astype(F32)
+        return total.astype(BF)
+
+    go(a1, 0)
+    go(b1, 0)
+    go(a1, 1)
+    go(b1, 1)
+    go(a1, 2)
+    for side in range(2):
+        for part in range(2):
+            rb[side, part * 4 : (part + 1) * 4] = b1[side].result(part)
+        direct(rb.at[side], bz.at[side], bz_send.at[side], bz_recv.at[side], NZ, Z, z_next)
+        a1[side].step(3)
+    for side in range(2):
+        for part in range(2):
+            ra[side, part * 2 : (part + 1) * 2] = a1[side].result(part)
+        direct(ra.at[side], ax.at[side], ax_send.at[side], ax_recv.at[side], NX, X, x_next)
+    my_piece = span(i_mine * 32, 32)
+    for side in range(2):
+        cols = slice(side * KV_W, (side + 1) * KV_W)
+        fb[:, cols] = collect(rb.at[side], bz.at[side], bz_recv.at[side], NZ, Z)
+    send_or_copy(self_b, fb, final.at[my_piece, :], fin_send.at[1], fin_recv, device(*target_b))
+    for side in range(2):
+        cols = slice(side * KV_W, (side + 1) * KV_W)
+        fa[:, cols] = collect(ra.at[side], ax.at[side], ax_recv.at[side], NX, X)
+    send_or_copy(self_a, fa, final.at[my_piece, :], fin_send.at[0], fin_recv, device(*target_a))
+
+    def sixty_four(member):
+        return final.at[span(member * 64, 64), :]
+
+    mine = sixty_four(seq)
+    wait_bytes(mine, fin_recv)
+    to_beside = remote(mine, mine, f2_send.at[0], f2_recv.at[0], beside)
+    to_partner = remote(mine, mine, f2_send.at[1], f2_recv.at[1], partner)
+    to_beside.start()
+    to_partner.start()
+    got = sixty_four((1 - low) * 2 + C)
+    wait_bytes(got, f2_recv.at[0])
+    passed = remote(got, got, f2_send.at[2], f2_recv.at[2], partner)
+    passed.start()
+    to_partner.wait_recv()
+    passed.wait_recv()
     for j in range(2):
         for what, out in ((0, key_out), (1, value_out)):
             first = (2 * j + what) * HD
             out[:, j * HD : (j + 1) * HD] = final[:, first : first + HD].astype(F32) * 0.25
 
     wait_bytes(query_grad, dq_recv)
-    exchange.wait_send()
+    for copy in exchanges.values():
+        copy.wait_send()
     for xs in range(NX):
         wait_sent(jnp.logical_and(same, X == xs), dq.at[xs], dq_send.at[xs])
     for quarter in range(4):
         wait_sent(seq == quarter, tokq.at[0], tok_send.at[quarter])
-    for part in range(2):
-        wait_sent(jnp.logical_and(same, X == 2 * C + part), raw.at[part], home_send.at[part])
-    for copy in sends + forwards:
+    for half in range(2):
+        for part in range(2):
+            wait_sent(
+                jnp.logical_and(same, X == 2 * C + part),
+                raw.at[part, pl.ds(half * HALF_ROWS, HALF_ROWS), :],
+                home_send.at[half, part],
+            )
+    for copy in sends + forwards + [to_beside, to_partner, passed]:
         copy.wait_send()
-    for each in (ring, a_first, b_first, a_next, b_next):
-        each.finish()
-    for is_self, src, sem in final_sends:
-        wait_sent(is_self, src, sem)
+    for ring in rings + a1 + b1:
+        ring.finish()
+    for copy in directs:
+        copy.wait_send()
+    wait_sent(self_a, fa, fin_send.at[0])
+    wait_sent(self_b, fb, fin_send.at[1])
 
 
 def back(dq, dkv, tokens, clip_masks):
-    def slots(steps, rows, cols):
-        return pltpu.VMEM((2, 2, steps, rows, cols), BF)
-
     wide = 2 * KV_W
     return pl.pallas_call(
         back_kernel,
@@ -646,56 +739,61 @@
             jax.ShapeDtypeStruct((256, KV_W), F32),
             jax.ShapeDtypeStruct((256, KV_W), F32),
         ),
-        in_specs=[ANY_SPEC] * 3 + [VMEM_SPEC],
+        in_specs=[ANY_SPEC] * 4,
         out_specs=(ANY_SPEC, VMEM_SPEC, VMEM_SPEC),
         scratch_shapes=[
-            pltpu.VMEM((16, BLK, KV_W), BF),
-            pltpu.VMEM((16, BLK, KV_W), BF),
-            slots(4, BLK, KV_W),
+            pltpu.VMEM((2, NZ, BLK, KV_W), BF),
+            pltpu.VMEM((2, NZ, BLK, KV_W), BF),
+            pltpu.VMEM((2, 2, 2, 4, HALF_ROWS, KV_W), BF),
             pltpu.VMEM((2, BLK, KV_W), BF),
             pltpu.VMEM((2, BLK, KV_W), BF),
+            pltpu.VMEM((2, 1, BLK, KV_W), jnp.int32),
             pltpu.VMEM((4, BLK, QUARTER), BF),
-            pltpu.VMEM((QUARTER, 4 * BLK), BF),
+            pltpu.VMEM((NZ, NX, 32, 4 * BLK), BF),
             pltpu.VMEM((2, 4 * BLK, wide), BF),
-            pltpu.VMEM((QUARTER, wide), BF),
-            pltpu.VMEM((QUARTER, wide), BF),
-            slots(4, 64, wide),
-            pltpu.VMEM((128, wide), BF),
-            slots(2, 16, wide),
+            pltpu.VMEM((2, NZ, NX, 32, KV_W), BF),
+            pltpu.VMEM((2, NZ, NX, 32, KV_W), BF),
+            pltpu.VMEM((2, 2, 2, 4, 2, 32, KV_W), BF),
+            pltpu.VMEM((2, NX, 32, KV_W), BF),
+            pltpu.VMEM((2, NX - 1, 32, KV_W), BF),
             pltpu.VMEM((32, wide), BF),
-            slots(2, 128, wide),
-            pltpu.VMEM((256, wide), BF),
-            slots(4, 16, wide),
+            pltpu.VMEM((2, 2, 2, 2, 4, 32, KV_W), BF),
+            pltpu.VMEM((2, NZ, 32, KV_W), BF),
+            pltpu.VMEM((2, NZ - 1, 32, KV_W), BF),
             pltpu.VMEM((32, wide), BF),
             pltpu.VMEM((256, wide), BF),
             DMA,
+            DMA,
+            DMA((8,)),
+            DMA((8,)),
+            DMA((2, 2, 2, 4)),
+            DMA((2, 2, 2, 4)),
+            DMA((2, 2)),
             DMA((2,)),
-            DMA((2, 2, 4)),
-            DMA((2, 2, 4)),
+            DMA((4,)),
+            DMA,
+            DMA((4,)),
+            DMA,
+            DMA((2, 3)),
+            DMA((2, 3)),
+            DMA((2, 3)),
+            DMA((2, 3)),
+            DMA((2, 2)),
+            DMA((2, 2, 2, 4)),
+            DMA((2, 2, 2, 4)),
+            DMA((2, NX - 1)),
+            DMA((2, NX - 1)),
+            DMA((2, 2, 2, 2)),
+            DMA((2, 2, 2, 2)),
+            DMA((2, NZ - 1)),
+            DMA((2, NZ - 1)),
             DMA((2,)),
-            DMA,
-            DMA((4,)),
-            DMA,
-            DMA((4,)),
             DMA,
             DMA((3,)),
             DMA((3,)),
-            DMA((3,)),
-            DMA((3,)),
-            DMA((2,)),
-            DMA((2, 2, 4)),
-            DMA((2, 2, 4)),
-            DMA((2, 2, 2)),
-            DMA((2, 2, 2)),
-            DMA((2, 2, 2)),
-            DMA((2, 2, 2)),
-            DMA((2, 2, 4)),
-            DMA((2, 2, 4)),
-            DMA((2, 2, 2)),
-            DMA,
         ],
         compiler_params=pltpu.CompilerParams(
-            collective_id=1, has_side_effects=True, vmem_limit_bytes=40 * 2**20
+            collective_id=1, has_side_effects=True, vmem_limit_bytes=VMEM_GRANT
         ),
         cost_estimate=pl.CostEstimate(flops=10**9, bytes_accessed=16 * 2**20, transcendentals=0),
     )(dq, dkv, tokens, clip_masks)

time: 176 us -> 152 us (0.86)
  Pallas kernels: 157 us -> 144 us
  local copies, waits for them, and re-layouts: 16.4 us -> 5.22 us
    pallas_call x1, Pallas kernels: 87.6 us -> 68.6 us  [back(): pl.pallas_call(back_kernel, name='back', out_shape=(jax.ShapeDtypeStruct(...]
    unnamed x29 -> x3, local copies, waits for them, and re-layouts: 16.4 us -> 5.22 us
    pallas_call x1, Pallas kernels: 24.3 us -> 29.8 us  [attention(): pl.pallas_call(attention_kernel, name='attention', out_shape=(jax.ShapeDt...]
where the time goes in v2:
time: 152 us; the launch traced here: 150 us
  Pallas kernels  144 us (95%)
  local copies, waits for them, and re-layouts  5.22 us (3%)
    pallas_call x1, Pallas kernels, back(): pl.pallas_call(back_kernel, name='back', out_shape=(jax.ShapeDtypeStruct(...  68.6 us
    pallas_call x1, Pallas kernels, front(): pl.pallas_call(front_kernel, name='front', out_shape=(jax.ShapeDtypeStruc...  45.4 us
    pallas_call x1, Pallas kernels, attention(): pl.pallas_call(attention_kernel, name='attention', out_shape=(jax.ShapeDt...  29.8 us
    unnamed x3, local copies, waits for them, and re-layouts  5.22 us

profile of v2, /device:TPU:71, one launch (start us, length us, event | category | flops | bytes accessed | tf_op | source)
XLA Modules:
  0.0 149.6 jit_solution(13847566713610289638)
XLA Ops:
  0.6 45.4 %front.1 = (bf16[4,128,512]{2,1,0:T(8,128)(2,1)}, bf16[4,128,512]{2,1,0:T(8,128)(2,1)}, bf16[32,128,256]{2,1,0:T(8,128)(2,1)}) custom-call(bf16[1,128,4096]{2,1,0:T(8,128)(2,1)} %tok.3, bf16[1,128,2048]{2,1,0:T(8,128)(2,1)} %q.1, bf16[1,128,2048]{2,1,0:T(8,128)(2,1)} %do.1, bf16[8192,256]{1,0:T(8,128)(2,1)} %kw.1, bf16[8192,256]{1,0:T(8,128)(2,1)} %vw.1, ...), custom_call_target="tpu_custom_call" | custom-call | flops 1000000000 | bytes 16777216 | tf_op jit(solution)/shard_map/front/pallas_call | solution.py:196
  46.0 29.8 %attention.1 = (bf16[4,128,512]{2,1,0:T(8,128)(2,1)}, bf16[4,8,128,256]{3,2,1,0:T(8,128)(2,1)}) custom-call(s32[32]{0:T(128)} %order.1, bf16[4,128,512]{2,1,0:T(8,128)(2,1)} %get-tuple-element.8.q, bf16[4,128,512]{2,1,0:T(8,128)(2,1)} %get-tuple-element.9.do, bf16[32,128,256]{2,1,0:T(8,128)(2,1)} %get-tuple-element.10.kv), custom_call_target="tpu_custom_call" | custom-call | flops 10000000000 | bytes 8388608 | tf_op jit(solution)/shard_map/attention/pallas_call | solution.py:356
  75.8 68.6 %back.1 = (bf16[1,128,2048]{2,1,0:T(8,128)(2,1)}, f32[256,256]{1,0:T(8,128)}, f32[256,256]{1,0:T(8,128)}) custom-call(bf16[4,128,512]{2,1,0:T(8,128)(2,1)} %get-tuple-element.11.dq, bf16[4,8,128,256]{3,2,1,0:T(8,128)(2,1)} %get-tuple-element.12.dkv, bf16[1,128,4096]{2,1,0:T(8,128)(2,1)} %tok.3, s32[2,1,128,256]{3,2,1,0:T(8,128)} %masks.1), custom_call_target="tpu_custom_call" | custom-call | flops 1000000000 | bytes 16777216 | tf_op jit(solution)/shard_map/back/pallas_call | solution.py:734
  144.4 1.9 %copy.14 = bf16[1,128,2048]{2,1,0:T(8,128)(2,1)} copy(bf16[1,128,2048]{2,1,0:T(8,128)(2,1)} %get-tuple-element.16) | data formatting | bytes 1048576
  146.2 1.7 %copy.15 = f32[256,256]{1,0:T(8,128)} copy(f32[256,256]{1,0:T(8,128)} %get-tuple-element.17) | data formatting | bytes 524288
  147.9 1.7 %copy.16 = f32[256,256]{1,0:T(8,128)} copy(f32[256,256]{1,0:T(8,128)} %get-tuple-element.18) | data formatting | bytes 524288

commit v3 on v2

--- a/solution.py
+++ b/solution.py
@@ -25,6 +25,7 @@
 F32 = jnp.float32
 MESH = pl.DeviceIdType.MESH
 VMEM_GRANT = 62 * 2**20
+BACK_GRANT = 52 * 2**20
 NT = (((1,), (1,)), ((), ()))
 NN = (((1,), (0,)), ((), ()))
 TN = (((0,), (0,)), ((), ()))
@@ -73,14 +74,15 @@
         wait_bytes(ref, send_sem)
 
 
-ROW_CHUNKS = 4
-CHUNK = BLK // ROW_CHUNKS
+CHUNKS = ((0, 16, True), (16, 32, True), (48, 32, True), (80, 32, True), (112, 16, False))
+IN_FLIGHT = 2
+ROW_CHUNKS = len(CHUNKS)
 
 
 def front_kernel(
     tok, q, do, kw, vw, codes_in, qx, dox, kv,
     codes, xbuf, wbuf, acc, kvst,
-    codes_sem, w_sem, own_sem, tok_send, tok_recv, q_send, q_recv, kv_send, kv_send0, kv_recv, fw_send, fw_recv,
+    codes_sem, w_sem, own_sem, tok_send, tok_recv, q_send, q_recv, kv_send, kv_send0, kv_recv, hop_send, fw_send, fw_recv,
 ):
     X, Y, Z, C = here()
     head = Y // 2
@@ -105,23 +107,19 @@
         @pl.when(jnp.logical_not(jnp.logical_and(same, X == xs)))
         def _(xs=xs):
             signal(device(xs, Y, Z, unit_core))
-    for part in range(2):
-        signal_x = 2 * C + part
-
-        @pl.when(jnp.logical_not(jnp.logical_and(same, X == signal_x)))
-        def _(signal_x=signal_x):
-            signal(device(signal_x, Y, Z, unit_core))
-
-        def far(step, carry, signal_x=signal_x):
-            signal(device(signal_x, Y, around(Z + step, NZ), unit_core))
-            return carry
-
-        lax.fori_loop(1, NZ, far, 0)
-    pl.semaphore_wait(pltpu.get_barrier_semaphore(), 22 - 2 * same.astype(jnp.int32))
-
-    for r in range(ROW_CHUNKS):
-        rows = pl.ds(r * CHUNK, CHUNK)
-        remote(tok.at[0, rows, :], xbuf.at[head, rows, :], tok_send.at[r], tok_recv.at[r], peer).start()
+    for delta in (1, -1, 2, -2):
+        zs = around(Z + delta, NZ)
+        signal(device(X, Y, zs, C))
+        for part in range(2):
+            signal(device(2 * C + part, Y, zs, unit_core))
+    pl.semaphore_wait(pltpu.get_barrier_semaphore(), 18 - same.astype(jnp.int32))
+
+    def token_copy(r):
+        rows = pl.ds(CHUNKS[r][0], CHUNKS[r][1])
+        return remote(tok.at[0, rows, :], xbuf.at[head, rows, :], tok_send.at[r], tok_recv.at[r], peer)
+
+    for r in range(IN_FLIGHT):
+        token_copy(r).start()
     for j in range(2):
         for c2 in range(NC):
             cols = pl.ds((j * 8 + c2 * 4) * HD, GROUP_COLS)
@@ -137,47 +135,72 @@
 
     mine = X * NZ + Z
 
+    def rows_of(r):
+        return pl.ds(CHUNKS[r][0], CHUNKS[r][1])
+
+    def blocks(r, count):
+        return kv.at[pl.ds(C * 16, count), rows_of(r), :]
+
+    def spread(r):
+        rows = rows_of(r)
+        deltas = (2, -2, 1, -1) if CHUNKS[r][2] else (4, 3, -3, 2, -2, 1, -1)
+        for j in range(2):
+            src = kvst.at[j, rows, :]
+            dst = kv.at[mine, rows, :]
+            for delta in deltas:
+                kind = {2: 0, -2: 1}.get(delta, 2) if CHUNKS[r][2] else 2
+                target = device(2 * C + j, Y, around(Z + delta, NZ), unit_core)
+                remote(src, dst, kv_send.at[r, j], kv_recv.at[r, kind], target).start()
+            is_self = jnp.logical_and(same, 2 * C + j == X)
+            send_or_copy(is_self, src, dst, kv_send0.at[r, j], kv_recv.at[r, 2], device(2 * C + j, Y, Z, unit_core))
+
+    def relay(r):
+        rows = rows_of(r)
+        for kind, sign in ((0, 1), (1, -1)):
+            wait_bytes(blocks(r, 2), kv_recv.at[r, kind])
+            source = around(Z - 2 * sign, NZ)
+            for part in range(2):
+                piece = kv.at[(2 * C + part) * NZ + source, rows, :]
+                for far in (2, 1) if part == kind else (1,):
+                    target = device(X, Y, around(Z + sign * far, NZ), C)
+                    remote(piece, piece, hop_send.at[r, kind], kv_recv.at[r, 2], target).start()
+
     def forward(r):
-        rows = pl.ds(r * CHUNK, CHUNK)
-        blocks = kv.at[pl.ds(C * 16, 16), rows, :]
-        wait_bytes(blocks, kv_recv.at[r])
-        copy = remote(blocks, blocks, fw_send.at[r], fw_recv.at[r], partner)
-        copy.start()
+        wait_bytes(blocks(r, 12 if CHUNKS[r][2] else 16), kv_recv.at[r, 2])
+        whole = blocks(r, 16)
+        remote(whole, whole, fw_send.at[r], fw_recv.at[r], partner).start()
 
     for r in range(ROW_CHUNKS):
-        rows = pl.ds(r * CHUNK, CHUNK)
+        rows = rows_of(r)
         wait_bytes(xbuf.at[1 - head, rows, :], tok_recv.at[r])
+        token_copy(r).wait_send()
+        if r + IN_FLIGHT < ROW_CHUNKS:
+            token_copy(r + IN_FLIGHT).start()
         both = acc[rows, :] + jnp.dot(xbuf[1 - head, rows, :], wbuf[1 - head], preferred_element_type=F32)
         for what in range(2):
             shift = NOISE_STEP * (codes[what, 0, rows, :].astype(F32) - NOISE_MIDDLE)
             value = (both[:, what * KV_W : (what + 1) * KV_W] + shift).astype(BF)
             for j in range(2):
                 kvst[j, rows, what * HD : (what + 1) * HD] = value[:, j * HD : (j + 1) * HD]
-        for j in range(2):
-            src = kvst.at[j, rows, :]
-            dst = kv.at[mine, rows, :]
-            is_self = jnp.logical_and(same, 2 * C + j == X)
-            send_or_copy(is_self, src, dst, kv_send0.at[r, j], kv_recv.at[r], device(2 * C + j, Y, Z, unit_core))
-
-            def far(step, carry, j=j, r=r, src=src, dst=dst):
-                target = device(2 * C + j, Y, around(Z + step, NZ), unit_core)
-                remote(src, dst, kv_send.at[r, j], kv_recv.at[r], target).start()
-                return carry
-
-            lax.fori_loop(1, NZ, far, 0)
-        if r:
-            forward(r - 1)
+        spread(r)
+        if r >= 1 and CHUNKS[r - 1][2]:
+            relay(r - 1)
+        if r >= 2:
+            forward(r - 2)
+    forward(ROW_CHUNKS - 2)
     forward(ROW_CHUNKS - 1)
 
     for r in range(ROW_CHUNKS):
-        rows = pl.ds(r * CHUNK, CHUNK)
+        rows = rows_of(r)
         wait_bytes(kv.at[pl.ds((1 - C) * 16, 16), rows, :], fw_recv.at[r])
-        wait_bytes(kv.at[pl.ds(C * 16, 16), rows, :], fw_send.at[r])
-        wait_bytes(xbuf.at[head, rows, :], tok_send.at[r])
+        wait_bytes(blocks(r, 16), fw_send.at[r])
         for j in range(2):
             is_self = jnp.logical_and(same, 2 * C + j == X)
             wait_sent(is_self, kvst.at[j, rows, :], kv_send0.at[r, j])
-            wait_bytes(kv.at[pl.ds(0, NZ - 1), rows, :], kv_send.at[r, j])
+            wait_bytes(blocks(r, 4 if CHUNKS[r][2] else 7), kv_send.at[r, j])
+        if CHUNKS[r][2]:
+            for kind in range(2):
+                wait_bytes(blocks(r, 3), hop_send.at[r, kind])
     wait_bytes(qx, q_recv.at[0])
     wait_bytes(dox, q_recv.at[1])
     for j in range(2):
@@ -218,7 +241,8 @@
             DMA((2,)),
             DMA((ROW_CHUNKS, 2)),
             DMA((ROW_CHUNKS, 2)),
-            DMA((ROW_CHUNKS,)),
+            DMA((ROW_CHUNKS, 3)),
+            DMA((ROW_CHUNKS, 2)),
             DMA((ROW_CHUNKS,)),
             DMA((ROW_CHUNKS,)),
         ],
@@ -236,7 +260,7 @@
 
 def attention_kernel(
     order, q, do, kv, dq_out, dkv_out,
-    kvb, qs, dos, stb, dpb, dk, dv, dqt, dkvb, kv_sem, q_sem, do_sem, out_sem,
+    kvb, qs, dos, stb, dpb, dk, dv, dqt, dkvb, block_at, kv_sem, q_sem, do_sem, out_sem,
 ):
     Z = lax.rem(lax.axis_index("ctx"), NZ)
 
@@ -245,6 +269,7 @@
 
     def load(block, carry):
         pltpu.make_async_copy(kv.at[block], kvb.at[at_place(block), :], kv_sem).start()
+        block_at[order[block]] = block
         return carry
 
     for x in range(NX):
@@ -338,16 +363,13 @@
         rows = pl.ds(pl.multiple_of(i * 256, 256), 256)
         dkvb[rows, :HD] = (dk[rows, :] * SCALE).astype(BF)
         dkvb[rows, HD:] = dv[rows, :].astype(BF)
+        for j in range(2):
+            block = block_at[2 * i + j]
+            src = dkvb.at[pl.ds(pl.multiple_of(i * 256 + j * BLK, BLK), BLK), :]
+            pltpu.make_async_copy(src, dkv_out.at[block // NZ, lax.rem(block, NZ)], out_sem).start()
         return carry
 
     lax.fori_loop(0, 16, finish, 0)
-
-    def store(block, carry):
-        dst = dkv_out.at[block // NZ, lax.rem(block, NZ)]
-        pltpu.make_async_copy(dkvb.at[at_place(block), :], dst, out_sem).start()
-        return carry
-
-    lax.fori_loop(0, BLOCKS, store, 0)
     wait_bytes(dkvb, out_sem)
 
 
@@ -372,6 +394,7 @@
             pltpu.VMEM((tokens, HD), F32),
             pltpu.VMEM((HD, ROWS), F32),
             pltpu.VMEM((tokens, KV_W), BF),
+            pltpu.SMEM((BLOCKS,), jnp.int32),
             DMA,
             DMA,
             DMA,
@@ -439,7 +462,7 @@
 
 def back_kernel(
     dq, dkv, tok, masks, query_grad, key_out, value_out,
-    own, other, z1, home_src, raw, mbuf, tokq, tokt, preall, wa, wb, az, ra, ax, fa, bx, rb, bz, fb, final,
+    own, other, z1, home_src, raw, mbuf, tokq, tokt, preall, wa, wb, az, ra, ax, bx, rb, bz, fin, final,
     own_sem, mask_sem, ex_send, ex_recv, z1_send, z1_recv, home_send, home_recv, tok_send, tok_recv, dq_send, dq_recv,
     pre_send, pre_recv, pfw_send, pfw_recv, core_sem,
     az_send, az_recv, ax_send, ax_recv, bx_send, bx_recv, bz_send, bz_recv,
@@ -471,8 +494,8 @@
     ways = (1, 3, 2)
     i_mine = X + 4 * lax.rem(Z, 2)
     member = i_mine // 2
-    target_a = (Y, member // 2, 4 * C + Z // 2, lax.rem(member, 2))
-    target_b = (Y, 2 + member // 2, 4 * C + Z // 2, lax.rem(member, 2))
+    target_a = (Y, 2 * head + member // 2, 4 * C + Z // 2, lax.rem(member, 2))
+    target_b = (Y, 2 * (1 - head) + member // 2, 4 * C + Z // 2, lax.rem(member, 2))
 
     def is_me(place):
         x, y, z, core = place
@@ -561,6 +584,8 @@
 
     load_mask.wait()
     sends = []
+    y_targets = (beside, y_next(around(2 * low - 1, NY)), y_next(2))
+    y_places = ((head, 1 - low), (1 - head, 1 - low), (1 - head, low))
 
     def my_rows(half):
         return span(seq * BLK + half * HALF_ROWS, HALF_ROWS)
@@ -575,10 +600,14 @@
                 first = (2 * j + what) * HD
                 preall[head, my_rows(half), first : first + HD] = jnp.where(mask, piece, jnp.zeros_like(piece))
         mine = preall.at[head, my_rows(half), :]
-        for i, by in enumerate(ways):
-            sends.append(remote(mine, mine, pre_send.at[half, i], pre_recv.at[half, i], y_next(by)))
+        sends.append(remote(mine, mine, core_sem.at[half, 0], core_sem.at[half, 1], partner))
+        sends[-1].start()
+        for i in range(2):
+            sends.append(remote(mine, mine, pre_send.at[half, i], pre_recv.at[half, i], y_targets[i]))
             sends[-1].start()
-        sends.append(remote(mine, mine, core_sem.at[half, 0], core_sem.at[half, 1], partner))
+    for half in range(2):
+        mine = preall.at[head, my_rows(half), :]
+        sends.append(remote(mine, mine, pre_send.at[half, 2], pre_recv.at[half, 2], y_targets[2]))
         sends[-1].start()
 
     wait_bytes(tokq, tok_recv)
@@ -586,62 +615,60 @@
         tokt[:, :, :, s * BLK : (s + 1) * BLK] = tokq[s].T.reshape(NZ, NX, 32, BLK)
 
     forwards = []
-    for half in range(2):
-        for i, by in enumerate(ways):
-            ys = around(Y + NY - by, NY)
-            start = (lax.rem(ys, 2) * 2 + C) * BLK + half * HALF_ROWS
-            piece = preall.at[ys // 2, span(start, HALF_ROWS), :]
+
+    def pass_on(i):
+        place, lows = y_places[i]
+        for half in range(2):
+            piece = preall.at[place, span((lows * 2 + C) * BLK + half * HALF_ROWS, HALF_ROWS), :]
             wait_bytes(piece, pre_recv.at[half, i])
             copy = remote(piece, piece, pfw_send.at[half, i], pfw_recv.at[half, i], partner)
             copy.start()
             forwards.append(copy)
+        return forwards[-2:]
+
+    passed_on = [pass_on(0), pass_on(1)]
     for half in range(2):
-        sends[half * 4 + 3].wait_recv()
-    for copy in forwards:
+        sends[half * 3].wait_recv()
+    for copy in passed_on[0]:
         copy.wait_recv()
 
     made = set()
 
-    def product(which, delta):
-        if (which, delta) in made:
+    def product(path, which, delta):
+        if (path, which, delta) in made:
             return
-        made.add((which, delta))
-        if which == 0:
+        made.add((path, which, delta))
+        cols = slice(path * KV_W, (path + 1) * KV_W)
+        if path == 0:
             t = around(Z + delta, NZ)
             rows = tokt[t].reshape(128, 4 * BLK)
         else:
             t = around(X + delta, NX)
             rows = tokt[:, t].reshape(256, 4 * BLK)
-        value = jnp.dot(rows, preall[which], preferred_element_type=F32).astype(BF)
-        for side in range(2):
-            half = value[:, side * KV_W : (side + 1) * KV_W]
-            if which == 0:
-                wa[side, t] = half.reshape(NX, 32, KV_W)
-            else:
-                wb[side, :, t] = half.reshape(NZ, 32, KV_W)
-
-    def a_own(side):
+        value = jnp.dot(rows, preall[around(head + which, 2), :, cols], preferred_element_type=F32).astype(BF)
+        if path == 0:
+            wa[which, t] = value.reshape(NX, 32, KV_W)
+        else:
+            wb[which, :, t] = value.reshape(NZ, 32, KV_W)
+
+    def a_own(which):
         def get(part, delta):
             delta = 4 if delta == -4 else delta
-            product(0, delta)
-            return wa.at[side, around(Z + delta, NZ), pl.ds(part * 2, 2)]
+            product(0, which, delta)
+            return wa.at[which, around(Z + delta, NZ), pl.ds(part * 2, 2)]
 
         return get
 
-    def b_own(side):
+    def b_own(which):
         def get(part, delta):
             delta = 2 if delta == -2 else delta
-            product(1, delta)
-            return wb.at[side, pl.ds(part * 4, 4), around(X + delta, NX)]
+            product(1, which, delta)
+            return wb.at[which, pl.ds(part * 4, 4), around(X + delta, NX)]
 
         return get
 
     a1 = [Ring(NZ, Z, z_next, a_own(s), az.at[s], az_send.at[s], az_recv.at[s]) for s in range(2)]
     b1 = [Ring(NX, X, x_next, b_own(s), bx.at[s], bx_send.at[s], bx_recv.at[s]) for s in range(2)]
-
-    def go(rings, step):
-        for ring in rings:
-            ring.step(step)
 
     directs = []
 
@@ -661,29 +688,43 @@
             total += slots[i].astype(F32)
         return total.astype(BF)
 
-    go(a1, 0)
-    go(b1, 0)
-    go(a1, 1)
-    go(b1, 1)
-    go(a1, 2)
-    for side in range(2):
+    def turn_a(which):
         for part in range(2):
-            rb[side, part * 4 : (part + 1) * 4] = b1[side].result(part)
-        direct(rb.at[side], bz.at[side], bz_send.at[side], bz_recv.at[side], NZ, Z, z_next)
-        a1[side].step(3)
-    for side in range(2):
+            ra[which, part * 2 : (part + 1) * 2] = a1[which].result(part)
+        direct(ra.at[which], ax.at[which], ax_send.at[which], ax_recv.at[which], NX, X, x_next)
+
+    def turn_b(which):
         for part in range(2):
-            ra[side, part * 2 : (part + 1) * 2] = a1[side].result(part)
-        direct(ra.at[side], ax.at[side], ax_send.at[side], ax_recv.at[side], NX, X, x_next)
-    my_piece = span(i_mine * 32, 32)
-    for side in range(2):
-        cols = slice(side * KV_W, (side + 1) * KV_W)
-        fb[:, cols] = collect(rb.at[side], bz.at[side], bz_recv.at[side], NZ, Z)
-    send_or_copy(self_b, fb, final.at[my_piece, :], fin_send.at[1], fin_recv, device(*target_b))
-    for side in range(2):
-        cols = slice(side * KV_W, (side + 1) * KV_W)
-        fa[:, cols] = collect(ra.at[side], ax.at[side], ax_recv.at[side], NX, X)
-    send_or_copy(self_a, fa, final.at[my_piece, :], fin_send.at[0], fin_recv, device(*target_a))
+            rb[which, part * 4 : (part + 1) * 4] = b1[which].result(part)
+        direct(rb.at[which], bz.at[which], bz_send.at[which], bz_recv.at[which], NZ, Z, z_next)
+
+    def deliver(which, is_self, target):
+        fin[which, :, KV_W:] = collect(rb.at[which], bz.at[which], bz_recv.at[which], NZ, Z)
+        fin[which, :, :KV_W] = collect(ra.at[which], ax.at[which], ax_recv.at[which], NX, X)
+        dst = final.at[span(i_mine * 32, 32), :]
+        send_or_copy(is_self, fin.at[which], dst, fin_send.at[which], fin_recv, device(*target))
+
+    a1[0].step(0)
+    b1[0].step(0)
+    passed_on.append(pass_on(2))
+    a1[0].step(1)
+    for copy in passed_on[1] + passed_on[2]:
+        copy.wait_recv()
+    a1[1].step(0)
+    b1[1].step(0)
+    b1[0].step(1)
+    a1[0].step(2)
+    a1[1].step(1)
+    b1[1].step(1)
+    turn_b(0)
+    a1[0].step(3)
+    a1[1].step(2)
+    turn_a(0)
+    turn_b(1)
+    a1[1].step(3)
+    deliver(0, self_a, target_a)
+    turn_a(1)
+    deliver(1, self_b, target_b)
 
     def sixty_four(member):
         return final.at[span(member * 64, 64), :]
@@ -725,8 +766,8 @@
         ring.finish()
     for copy in directs:
         copy.wait_send()
-    wait_sent(self_a, fa, fin_send.at[0])
-    wait_sent(self_b, fb, fin_send.at[1])
+    wait_sent(self_a, fin.at[0], fin_send.at[0])
+    wait_sent(self_b, fin.at[1], fin_send.at[1])
 
 
 def back(dq, dkv, tokens, clip_masks):
@@ -756,11 +797,10 @@
             pltpu.VMEM((2, 2, 2, 4, 2, 32, KV_W), BF),
             pltpu.VMEM((2, NX, 32, KV_W), BF),
             pltpu.VMEM((2, NX - 1, 32, KV_W), BF),
-            pltpu.VMEM((32, wide), BF),
             pltpu.VMEM((2, 2, 2, 2, 4, 32, KV_W), BF),
             pltpu.VMEM((2, NZ, 32, KV_W), BF),
             pltpu.VMEM((2, NZ - 1, 32, KV_W), BF),
-            pltpu.VMEM((32, wide), BF),
+            pltpu.VMEM((2, 32, wide), BF),
             pltpu.VMEM((256, wide), BF),
             DMA,
             DMA,
@@ -793,7 +833,7 @@
             DMA((3,)),
         ],
         compiler_params=pltpu.CompilerParams(
-            collective_id=1, has_side_effects=True, vmem_limit_bytes=VMEM_GRANT
+            collective_id=1, has_side_effects=True, vmem_limit_bytes=BACK_GRANT
         ),
         cost_estimate=pl.CostEstimate(flops=10**9, bytes_accessed=16 * 2**20, transcendentals=0),
     )(dq, dkv, tokens, clip_masks)

time: 152 us -> 144 us (0.947); the launches traced: 150 us -> 144 us
  Pallas kernels: 144 us -> 140 us
  local copies, waits for them, and re-layouts: 5.22 us -> 3.24 us
    pallas_call x1, Pallas kernels: 29.8 us -> 22.6 us  [attention(): pl.pallas_call(attention_kernel, name='attention', out_shape=(jax.ShapeDt...]
    pallas_call x1, Pallas kernels: 68.6 us -> 73.3 us  [back(): pl.pallas_call(back_kernel, name='back', out_shape=(jax.ShapeDtypeStruct(...]
    unnamed x3 -> x7, local copies, waits for them, and re-layouts: 5.22 us -> 3.24 us
    pallas_call x1, Pallas kernels: 45.4 us -> 43.8 us  [front(): pl.pallas_call(front_kernel, name='front', out_shape=(jax.ShapeDtypeStruc...]
where the time goes in v3:
time: 144 us
  Pallas kernels  140 us (97%)
  local copies, waits for them, and re-layouts  3.24 us (2%)
    pallas_call x1, Pallas kernels, back(): pl.pallas_call(back_kernel, name='back', out_shape=(jax.ShapeDtypeStruct(...  73.3 us
    pallas_call x1, Pallas kernels, front(): pl.pallas_call(front_kernel, name='front', out_shape=(jax.ShapeDtypeStruc...  43.8 us
    pallas_call x1, Pallas kernels, attention(): pl.pallas_call(attention_kernel, name='attention', out_shape=(jax.ShapeDt...  22.6 us
    unnamed x7, local copies, waits for them, and re-layouts  3.24 us

profile of v3, /device:TPU:71, one launch (start us, length us, event | category | flops | bytes accessed | tf_op | source)
XLA Modules:
  0.0 143.6 jit_solution(691501857224555055)
XLA Ops:
  0.6 43.8 %front.1 = (bf16[4,128,512]{2,1,0:T(8,128)(2,1)}, bf16[4,128,512]{2,1,0:T(8,128)(2,1)}, bf16[32,128,256]{2,1,0:T(8,128)(2,1)}) custom-call(bf16[1,128,4096]{2,1,0:T(8,128)(2,1)} %tok.3, bf16[1,128,2048]{2,1,0:T(8,128)(2,1)} %q.1, bf16[1,128,2048]{2,1,0:T(8,128)(2,1)} %do.1, bf16[8192,256]{1,0:T(8,128)(2,1)} %kw.1, bf16[8192,256]{1,0:T(8,128)(2,1)} %vw.1, ...), custom_call_target="tpu_custom_call" | custom-call | flops 1000000000 | bytes 16777216 | tf_op jit(solution)/shard_map/front/pallas_call | solution.py:219
  44.5 0.0 copy-start.1
  44.5 22.6 %attention.1 = (bf16[4,128,512]{2,1,0:T(8,128)(2,1)}, bf16[4,8,128,256]{3,2,1,0:T(8,128)(2,1)}) custom-call(s32[32]{0:T(128)} %order.1, bf16[4,128,512]{2,1,0:T(8,128)(2,1)} %get-tuple-element.8.q, bf16[4,128,512]{2,1,0:T(8,128)(2,1)} %get-tuple-element.9.do, bf16[32,128,256]{2,1,0:T(8,128)(2,1)} %get-tuple-element.10.kv), custom_call_target="tpu_custom_call" | custom-call | flops 10000000000 | bytes 8388608 | tf_op jit(solution)/shard_map/attention/pallas_call | solution.py:378
  67.1 0.0 copy-done.1
  67.1 0.0 copy-start
  67.1 1.0 copy-done
  68.1 73.3 %back.1 = (bf16[1,128,2048]{2,1,0:T(8,128)(2,1)S(1)}, f32[256,256]{1,0:T(8,128)S(1)}, f32[256,256]{1,0:T(8,128)S(1)}) custom-call(bf16[4,128,512]{2,1,0:T(8,128)(2,1)S(1)} %copy-done, bf16[4,8,128,256]{3,2,1,0:T(8,128)(2,1)} %get-tuple-element.12.dkv, bf16[1,128,4096]{2,1,0:T(8,128)(2,1)} %tok.3, s32[2,1,128,256]{3,2,1,0:T(8,128)S(1)} %copy-done.1), custom_call_target="tpu_custom_call" | custom-call | flops 1000000000 | bytes 16777216 | tf_op jit(solution)/shard_map/back/pallas_call | solution.py:775
  141.4 0.8 copy.14
  142.2 0.7 copy.15
  142.9 0.7 copy.16
Async XLA Ops:
  44.5 22.6 %copy-start.1 = (s32[2,1,128,256]{3,2,1,0:T(8,128)S(1)}, s32[2,1,128,256]{3,2,1,0:T(8,128)}, u32[]{:S(2)}) copy-start(s32[2,1,128,256]{3,2,1,0:T(8,128)} %masks.1) | copy-start | bytes 786436
  67.1 1.0 copy-start

commit v4 on v3

--- a/solution.py
+++ b/solution.py
@@ -25,6 +25,7 @@
 F32 = jnp.float32
 MESH = pl.DeviceIdType.MESH
 VMEM_GRANT = 62 * 2**20
+ATTENTION_GRANT = 53 * 2**20
 BACK_GRANT = 52 * 2**20
 NT = (((1,), (1,)), ((), ()))
 NN = (((1,), (0,)), ((), ()))
@@ -254,7 +255,7 @@
 
 
 KEYS = 256
-LEVELS = (4, 2, 1)
+LEVELS = (8, 4, 2, 1)
 ROWS = 4 * BLK
 
 
@@ -400,7 +401,7 @@
             DMA,
             DMA,
         ],
-        compiler_params=pltpu.CompilerParams(vmem_limit_bytes=VMEM_GRANT),
+        compiler_params=pltpu.CompilerParams(vmem_limit_bytes=ATTENTION_GRANT),
         cost_estimate=pl.CostEstimate(flops=10**10, bytes_accessed=8 * 2**20, transcendentals=10**7),
     )(block_order, qx, dox, kv)
 
@@ -457,6 +458,8 @@
 
 
 HALF_ROWS = BLK // 2
+RINGS = 4
+RING_ROWS = BLK // RINGS
 DELTAS = (4, 3, -3, 2, -2, 1, -1, 0)
 
 
@@ -493,15 +496,16 @@
 
     ways = (1, 3, 2)
     i_mine = X + 4 * lax.rem(Z, 2)
-    member = i_mine // 2
-    target_a = (Y, 2 * head + member // 2, 4 * C + Z // 2, lax.rem(member, 2))
-    target_b = (Y, 2 * (1 - head) + member // 2, 4 * C + Z // 2, lax.rem(member, 2))
+    targets = [
+        [(Y, 2 * around(head + which, 2) + lows, 4 * C + Z // 2, lax.rem(Z, 2)) for lows in range(2)]
+        for which in range(2)
+    ]
 
     def is_me(place):
         x, y, z, core = place
         return jnp.logical_and(jnp.logical_and(x == X, y == Y), jnp.logical_and(z == Z, core == C))
 
-    self_a, self_b = is_me(target_a), is_me(target_b)
+    is_final = [[is_me(target) for target in pair] for pair in targets]
 
     signal(partner)
     for xs in range(2):
@@ -554,23 +558,23 @@
         for part in range(2):
             own[part, t] = (own[part, t].astype(F32) + other[part, t].astype(F32)).astype(BF)
 
-    def own_part(half):
+    def own_part(i):
         def get(part, delta):
             prepare(4 if delta == -4 else delta)
-            return own.at[part, around(Z + delta, NZ), pl.ds(half * HALF_ROWS, HALF_ROWS), :]
+            return own.at[part, around(Z + delta, NZ), pl.ds(i * RING_ROWS, RING_ROWS), :]
 
         return get
 
-    rings = [
-        Ring(NZ, Z, z_next, own_part(half), z1.at[half], z1_send.at[half], z1_recv.at[half]) for half in range(2)
-    ]
+    rings = [Ring(NZ, Z, z_next, own_part(i), z1.at[i], z1_send.at[i], z1_recv.at[i]) for i in range(RINGS)]
     for step in range(NZ // 2):
         for ring in rings:
             ring.step(step)
-    for half, ring in enumerate(rings):
+    for half in range(2):
         rows = pl.ds(half * HALF_ROWS, HALF_ROWS)
+        for i in range(half * RINGS // 2, (half + 1) * RINGS // 2):
+            for part in range(2):
+                home_src[part, i * RING_ROWS : (i + 1) * RING_ROWS, :] = rings[i].result(part)
         for part in range(2):
-            home_src[part, rows, :] = ring.result(part)
             xs = 2 * C + part
             is_self = jnp.logical_and(same, X == xs)
             send_or_copy(
@@ -698,11 +702,19 @@
             rb[which, part * 4 : (part + 1) * 4] = b1[which].result(part)
         direct(rb.at[which], bz.at[which], bz_send.at[which], bz_recv.at[which], NZ, Z, z_next)
 
-    def deliver(which, is_self, target):
+    def deliver(which):
         fin[which, :, KV_W:] = collect(rb.at[which], bz.at[which], bz_recv.at[which], NZ, Z)
         fin[which, :, :KV_W] = collect(ra.at[which], ax.at[which], ax_recv.at[which], NX, X)
         dst = final.at[span(i_mine * 32, 32), :]
-        send_or_copy(is_self, fin.at[which], dst, fin_send.at[which], fin_recv, device(*target))
+        for lows in range(2):
+            send_or_copy(
+                is_final[which][lows],
+                fin.at[which],
+                dst,
+                fin_send.at[which, lows],
+                fin_recv,
+                device(*targets[which][lows]),
+            )
 
     a1[0].step(0)
     b1[0].step(0)
@@ -722,25 +734,15 @@
     turn_a(0)
     turn_b(1)
     a1[1].step(3)
-    deliver(0, self_a, target_a)
+    deliver(0)
     turn_a(1)
-    deliver(1, self_b, target_b)
-
-    def sixty_four(member):
-        return final.at[span(member * 64, 64), :]
-
-    mine = sixty_four(seq)
+    deliver(1)
+
+    mine = final.at[span(C * BLK, BLK), :]
     wait_bytes(mine, fin_recv)
-    to_beside = remote(mine, mine, f2_send.at[0], f2_recv.at[0], beside)
-    to_partner = remote(mine, mine, f2_send.at[1], f2_recv.at[1], partner)
-    to_beside.start()
+    to_partner = remote(mine, mine, f2_send, f2_recv, partner)
     to_partner.start()
-    got = sixty_four((1 - low) * 2 + C)
-    wait_bytes(got, f2_recv.at[0])
-    passed = remote(got, got, f2_send.at[2], f2_recv.at[2], partner)
-    passed.start()
     to_partner.wait_recv()
-    passed.wait_recv()
     for j in range(2):
         for what, out in ((0, key_out), (1, value_out)):
             first = (2 * j + what) * HD
@@ -760,14 +762,15 @@
                 raw.at[part, pl.ds(half * HALF_ROWS, HALF_ROWS), :],
                 home_send.at[half, part],
             )
-    for copy in sends + forwards + [to_beside, to_partner, passed]:
+    for copy in sends + forwards + [to_partner]:
         copy.wait_send()
     for ring in rings + a1 + b1:
         ring.finish()
     for copy in directs:
         copy.wait_send()
-    wait_sent(self_a, fin.at[0], fin_send.at[0])
-    wait_sent(self_b, fin.at[1], fin_send.at[1])
+    for which in range(2):
+        for lows in range(2):
+            wait_sent(is_final[which][lows], fin.at[which], fin_send.at[which, lows])
 
 
 def back(dq, dkv, tokens, clip_masks):
@@ -785,7 +788,7 @@
         scratch_shapes=[
             pltpu.VMEM((2, NZ, BLK, KV_W), BF),
             pltpu.VMEM((2, NZ, BLK, KV_W), BF),
-            pltpu.VMEM((2, 2, 2, 4, HALF_ROWS, KV_W), BF),
+            pltpu.VMEM((RINGS, 2, 2, 4, RING_ROWS, KV_W), BF),
             pltpu.VMEM((2, BLK, KV_W), BF),
             pltpu.VMEM((2, BLK, KV_W), BF),
             pltpu.VMEM((2, 1, BLK, KV_W), jnp.int32),
@@ -806,8 +809,8 @@
             DMA,
             DMA((8,)),
             DMA((8,)),
-            DMA((2, 2, 2, 4)),
-            DMA((2, 2, 2, 4)),
+            DMA((RINGS, 2, 2, 4)),
+            DMA((RINGS, 2, 2, 4)),
             DMA((2, 2)),
             DMA((2,)),
             DMA((4,)),
@@ -827,10 +830,10 @@
             DMA((2, 2, 2, 2)),
             DMA((2, NZ - 1)),
             DMA((2, NZ - 1)),
-            DMA((2,)),
-            DMA,
-            DMA((3,)),
-            DMA((3,)),
+            DMA((2, 2)),
+            DMA,
+            DMA,
+            DMA,
         ],
         compiler_params=pltpu.CompilerParams(
             collective_id=1, has_side_effects=True, vmem_limit_bytes=BACK_GRANT

time: 144 us -> 141 us (0.979)
  Pallas kernels: 140 us -> 137 us
    pallas_call x1, Pallas kernels: 22.6 us -> 18 us  [attention(): pl.pallas_call(attention_kernel, name='attention', out_shape=(jax.ShapeDt...]
    pallas_call x1, Pallas kernels: 73.3 us -> 75.5 us  [back(): pl.pallas_call(back_kernel, name='back', out_shape=(jax.ShapeDtypeStruct(...]
where the time goes in v4:
time: 141 us; the launch traced here: 140 us
  Pallas kernels  137 us (97%)
  local copies, waits for them, and re-layouts  2.21 us (2%)
    pallas_call x1, Pallas kernels, back(): pl.pallas_call(back_kernel, name='back', out_shape=(jax.ShapeDtypeStruct(...  75.5 us
    pallas_call x1, Pallas kernels, front(): pl.pallas_call(front_kernel, name='front', out_shape=(jax.ShapeDtypeStruc...  43.8 us
    pallas_call x1, Pallas kernels, attention(): pl.pallas_call(attention_kernel, name='attention', out_shape=(jax.ShapeDt...  18 us

profile of v4, /device:TPU:71, one launch (start us, length us, event | category | flops | bytes accessed | tf_op | source)
XLA Modules:
  0.0 140.2 jit_solution(2593642801731471202)
XLA Ops:
  0.6 0.0 copy-start.1
  0.6 43.8 %front.1 = (bf16[4,128,512]{2,1,0:T(8,128)(2,1)}, bf16[4,128,512]{2,1,0:T(8,128)(2,1)}, bf16[32,128,256]{2,1,0:T(8,128)(2,1)}) custom-call(bf16[1,128,4096]{2,1,0:T(8,128)(2,1)} %tok.3, bf16[1,128,2048]{2,1,0:T(8,128)(2,1)} %q.1, bf16[1,128,2048]{2,1,0:T(8,128)(2,1)} %do.1, bf16[8192,256]{1,0:T(8,128)(2,1)} %kw.1, bf16[8192,256]{1,0:T(8,128)(2,1)} %vw.1, ...), custom_call_target="tpu_custom_call" | custom-call | flops 1000000000 | bytes 16777216 | tf_op jit(solution)/shard_map/front/pallas_call | solution.py:220
  44.5 0.0 copy-done.1
  44.5 0.0 copy-start
  44.5 18.0 %attention.1 = (bf16[4,128,512]{2,1,0:T(8,128)(2,1)S(1)}, bf16[4,8,128,256]{3,2,1,0:T(8,128)(2,1)}) custom-call(s32[32]{0:T(128)S(1)} %copy-done.1, bf16[4,128,512]{2,1,0:T(8,128)(2,1)} %get-tuple-element.8.q, bf16[4,128,512]{2,1,0:T(8,128)(2,1)} %get-tuple-element.9.do, bf16[32,128,256]{2,1,0:T(8,128)(2,1)} %get-tuple-element.10.kv), custom_call_target="tpu_custom_call" | custom-call | flops 10000000000 | bytes 8388608 | tf_op jit(solution)/shard_map/attention/pallas_call | solution.py:379
  62.5 0.0 copy-done
  62.5 75.5 %back.1 = (bf16[1,128,2048]{2,1,0:T(8,128)(2,1)S(1)}, f32[256,256]{1,0:T(8,128)S(1)}, f32[256,256]{1,0:T(8,128)S(1)}) custom-call(bf16[4,128,512]{2,1,0:T(8,128)(2,1)S(1)} %get-tuple-element.11.dq, bf16[4,8,128,256]{3,2,1,0:T(8,128)(2,1)} %get-tuple-element.12.dkv, bf16[1,128,4096]{2,1,0:T(8,128)(2,1)} %tok.3, s32[2,1,128,256]{3,2,1,0:T(8,128)S(1)} %copy-done), custom_call_target="tpu_custom_call" | custom-call | flops 1000000000 | bytes 16777216 | tf_op jit(solution)/shard_map/back/pallas_call | solution.py:778
  138.0 0.8 copy.14
  138.8 0.7 copy.15
  139.5 0.7 copy.16
Async XLA Ops:
  0.6 43.8 %copy-start.1 = (s32[32]{0:T(128)S(1)}, s32[32]{0:T(128)}, u32[]{:S(2)}) copy-start(s32[32]{0:T(128)} %order.1) | copy-start | bytes 388
  44.5 18.0 %copy-start = (s32[2,1,128,256]{3,2,1,0:T(8,128)S(1)}, s32[2,1,128,256]{3,2,1,0:T(8,128)}, u32[]{:S(2)}) copy-start(s32[2,1,128,256]{3,2,1,0:T(8,128)} %masks.1) | copy-start | bytes 786436

commit v5 on v4

--- a/solution.py
+++ b/solution.py
@@ -92,16 +92,6 @@
     peer = device(X, around(Y + 2, NY), Z, C)
     partner = device(X, Y, Z, 1 - C)
 
-    loads = [pltpu.make_async_copy(codes_in, codes, codes_sem)]
-    for half in range(2):
-        rows = pl.ds(half * HALF_D, HALF_D)
-        loads.append(pltpu.make_async_copy(kw.at[rows, :], wbuf.at[half, :, pl.ds(0, KV_W)], w_sem.at[half, 0]))
-        loads.append(pltpu.make_async_copy(vw.at[rows, :], wbuf.at[half, :, pl.ds(KV_W, KV_W)], w_sem.at[half, 1]))
-    own_x = pltpu.make_async_copy(tok.at[0], xbuf.at[head], own_sem)
-    own_x.start()
-    for load in loads:
-        load.start()
-
     signal(peer)
     signal(partner)
     for xs in range(NX):
@@ -113,6 +103,16 @@
         signal(device(X, Y, zs, C))
         for part in range(2):
             signal(device(2 * C + part, Y, zs, unit_core))
+    loads = [pltpu.make_async_copy(codes_in, codes, codes_sem)]
+    for half in range(2):
+        rows = pl.ds(half * HALF_D, HALF_D)
+        loads.append(pltpu.make_async_copy(kw.at[rows, :], wbuf.at[half, :, pl.ds(0, KV_W)], w_sem.at[half, 0]))
+        loads.append(pltpu.make_async_copy(vw.at[rows, :], wbuf.at[half, :, pl.ds(KV_W, KV_W)], w_sem.at[half, 1]))
+    own_x = pltpu.make_async_copy(tok.at[0], xbuf.at[head], own_sem)
+    own_x.start()
+    for load in loads:
+        load.start()
+
     pl.semaphore_wait(pltpu.get_barrier_semaphore(), 18 - same.astype(jnp.int32))
 
     def token_copy(r):
@@ -480,11 +480,6 @@
     beside = device(X, 2 * head + 1 - low, Z, C)
     seq = low * 2 + C
 
-    load_own = pltpu.make_async_copy(dkv.at[pl.ds(C * 2, 2)], own, own_sem)
-    load_own.start()
-    load_mask = pltpu.make_async_copy(masks, mbuf, mask_sem)
-    load_mask.start()
-
     def z_next(sign):
         return device(X, Y, around(Z + sign, NZ), C)
 
@@ -521,6 +516,10 @@
     for by in ways:
         signal(y_next(by))
     signal(device(around(X + 2, NX), Y, Z, C))
+    load_own = pltpu.make_async_copy(dkv.at[pl.ds(C * 2, 2)], own, own_sem)
+    load_own.start()
+    load_mask = pltpu.make_async_copy(masks, mbuf, mask_sem)
+    load_mask.start()
     pl.semaphore_wait(pltpu.get_barrier_semaphore(), 15 - same.astype(jnp.int32))
 
     exchanges = {}
@@ -717,25 +716,25 @@
             )
 
     a1[0].step(0)
-    b1[0].step(0)
     passed_on.append(pass_on(2))
     a1[0].step(1)
     for copy in passed_on[1] + passed_on[2]:
         copy.wait_recv()
     a1[1].step(0)
+    b1[0].step(0)
     b1[1].step(0)
-    b1[0].step(1)
     a1[0].step(2)
     a1[1].step(1)
+    b1[0].step(1)
+    a1[0].step(3)
+    a1[1].step(2)
     b1[1].step(1)
     turn_b(0)
-    a1[0].step(3)
-    a1[1].step(2)
     turn_a(0)
+    a1[1].step(3)
     turn_b(1)
-    a1[1].step(3)
+    turn_a(1)
     deliver(0)
-    turn_a(1)
     deliver(1)
 
     mine = final.at[span(C * BLK, BLK), :]

time: 141 us -> 140 us (level)
    pallas_call x1, Pallas kernels: 75.5 us -> 66 us  [back(): pl.pallas_call(back_kernel, name='back', out_shape=(jax.ShapeDtypeStruct(...]
    pallas_call x1, Pallas kernels: 18 us -> 26 us  [attention(): pl.pallas_call(attention_kernel, name='attention', out_shape=(jax.ShapeDt...]
where the time goes in v5:
time: 140 us; the launch traced here: 139 us
  Pallas kernels  136 us (97%)
  local copies, waits for them, and re-layouts  2.21 us (2%)
    pallas_call x1, Pallas kernels, back(): pl.pallas_call(back_kernel, name='back', out_shape=(jax.ShapeDtypeStruct(...  66 us
    pallas_call x1, Pallas kernels, front(): pl.pallas_call(front_kernel, name='front', out_shape=(jax.ShapeDtypeStruc...  43.8 us
    pallas_call x1, Pallas kernels, attention(): pl.pallas_call(attention_kernel, name='attention', out_shape=(jax.ShapeDt...  26 us

profile of v5, /device:TPU:71, one launch (start us, length us, event | category | flops | bytes accessed | tf_op | source)
XLA Modules:
  0.0 138.7 jit_solution(4990862060746311770)
XLA Ops:
  0.6 0.0 copy-start.1
  0.6 43.8 %front.1 = (bf16[4,128,512]{2,1,0:T(8,128)(2,1)}, bf16[4,128,512]{2,1,0:T(8,128)(2,1)}, bf16[32,128,256]{2,1,0:T(8,128)(2,1)}) custom-call(bf16[1,128,4096]{2,1,0:T(8,128)(2,1)} %tok.3, bf16[1,128,2048]{2,1,0:T(8,128)(2,1)} %q.1, bf16[1,128,2048]{2,1,0:T(8,128)(2,1)} %do.1, bf16[8192,256]{1,0:T(8,128)(2,1)} %kw.1, bf16[8192,256]{1,0:T(8,128)(2,1)} %vw.1, ...), custom_call_target="tpu_custom_call" | custom-call | flops 1000000000 | bytes 16777216 | tf_op jit(solution)/shard_map/front/pallas_call | solution.py:220
  44.5 0.0 copy-done.1
  44.5 0.0 copy-start
  44.5 26.0 %attention.1 = (bf16[4,128,512]{2,1,0:T(8,128)(2,1)S(1)}, bf16[4,8,128,256]{3,2,1,0:T(8,128)(2,1)}) custom-call(s32[32]{0:T(128)S(1)} %copy-done.1, bf16[4,128,512]{2,1,0:T(8,128)(2,1)} %get-tuple-element.8.q, bf16[4,128,512]{2,1,0:T(8,128)(2,1)} %get-tuple-element.9.do, bf16[32,128,256]{2,1,0:T(8,128)(2,1)} %get-tuple-element.10.kv), custom_call_target="tpu_custom_call" | custom-call | flops 10000000000 | bytes 8388608 | tf_op jit(solution)/shard_map/attention/pallas_call | solution.py:379
  70.4 0.0 copy-done
  70.5 66.0 %back.1 = (bf16[1,128,2048]{2,1,0:T(8,128)(2,1)S(1)}, f32[256,256]{1,0:T(8,128)S(1)}, f32[256,256]{1,0:T(8,128)S(1)}) custom-call(bf16[4,128,512]{2,1,0:T(8,128)(2,1)S(1)} %get-tuple-element.11.dq, bf16[4,8,128,256]{3,2,1,0:T(8,128)(2,1)} %get-tuple-element.12.dkv, bf16[1,128,4096]{2,1,0:T(8,128)(2,1)} %tok.3, s32[2,1,128,256]{3,2,1,0:T(8,128)S(1)} %copy-done), custom_call_target="tpu_custom_call" | custom-call | flops 1000000000 | bytes 16777216 | tf_op jit(solution)/shard_map/back/pallas_call | solution.py:777
  136.5 0.8 copy.14
  137.3 0.7 copy.15
  138.0 0.7 copy.16
Async XLA Ops:
  0.6 43.8 %copy-start.1 = (s32[32]{0:T(128)S(1)}, s32[32]{0:T(128)}, u32[]{:S(2)}) copy-start(s32[32]{0:T(128)} %order.1) | copy-start | bytes 388
  44.5 26.0 %copy-start = (s32[2,1,128,256]{3,2,1,0:T(8,128)S(1)}, s32[2,1,128,256]{3,2,1,0:T(8,128)}, u32[]{:S(2)}) copy-start(s32[2,1,128,256]{3,2,1,0:T(8,128)} %masks.1) | copy-start | bytes 786436

commit v6 on v5

--- a/solution.py
+++ b/solution.py
@@ -629,7 +629,7 @@
             forwards.append(copy)
         return forwards[-2:]
 
-    passed_on = [pass_on(0), pass_on(1)]
+    passed_on = [pass_on(0)]
     for half in range(2):
         sends[half * 3].wait_recv()
     for copy in passed_on[0]:
@@ -716,6 +716,7 @@
             )
 
     a1[0].step(0)
+    passed_on.append(pass_on(1))
     passed_on.append(pass_on(2))
     a1[0].step(1)
     for copy in passed_on[1] + passed_on[2]:

time: 140 us -> 138 us (0.986)
    pallas_call x1, Pallas kernels: 26 us -> 18.8 us  [attention(): pl.pallas_call(attention_kernel, name='attention', out_shape=(jax.ShapeDt...]
    pallas_call x1, Pallas kernels: 66 us -> 71.9 us  [back(): pl.pallas_call(back_kernel, name='back', out_shape=(jax.ShapeDtypeStruct(...]
where the time goes in v6:
time: 138 us; the launch traced here: 137 us
  Pallas kernels  135 us (98%)
  local copies, waits for them, and re-layouts  2.21 us (2%)
    pallas_call x1, Pallas kernels, back(): pl.pallas_call(back_kernel, name='back', out_shape=(jax.ShapeDtypeStruct(...  71.9 us
    pallas_call x1, Pallas kernels, front(): pl.pallas_call(front_kernel, name='front', out_shape=(jax.ShapeDtypeStruc...  43.8 us
    pallas_call x1, Pallas kernels, attention(): pl.pallas_call(attention_kernel, name='attention', out_shape=(jax.ShapeDt...  18.8 us

profile of v6, /device:TPU:71, one launch (start us, length us, event | category | flops | bytes accessed | tf_op | source)
XLA Modules:
  0.0 137.4 jit_solution(9260138248802366752)
XLA Ops:
  0.6 0.0 copy-start.1
  0.6 43.8 %front.1 = (bf16[4,128,512]{2,1,0:T(8,128)(2,1)}, bf16[4,128,512]{2,1,0:T(8,128)(2,1)}, bf16[32,128,256]{2,1,0:T(8,128)(2,1)}) custom-call(bf16[1,128,4096]{2,1,0:T(8,128)(2,1)} %tok.3, bf16[1,128,2048]{2,1,0:T(8,128)(2,1)} %q.1, bf16[1,128,2048]{2,1,0:T(8,128)(2,1)} %do.1, bf16[8192,256]{1,0:T(8,128)(2,1)} %kw.1, bf16[8192,256]{1,0:T(8,128)(2,1)} %vw.1, ...), custom_call_target="tpu_custom_call" | custom-call | flops 1000000000 | bytes 16777216 | tf_op jit(solution)/shard_map/front/pallas_call | solution.py:220
  44.5 0.0 copy-done.1
  44.5 0.0 copy-start
  44.5 18.8 %attention.1 = (bf16[4,128,512]{2,1,0:T(8,128)(2,1)S(1)}, bf16[4,8,128,256]{3,2,1,0:T(8,128)(2,1)}) custom-call(s32[32]{0:T(128)S(1)} %copy-done.1, bf16[4,128,512]{2,1,0:T(8,128)(2,1)} %get-tuple-element.8.q, bf16[4,128,512]{2,1,0:T(8,128)(2,1)} %get-tuple-element.9.do, bf16[32,128,256]{2,1,0:T(8,128)(2,1)} %get-tuple-element.10.kv), custom_call_target="tpu_custom_call" | custom-call | flops 10000000000 | bytes 8388608 | tf_op jit(solution)/shard_map/attention/pallas_call | solution.py:379
  63.2 0.0 copy-done
  63.3 71.9 %back.1 = (bf16[1,128,2048]{2,1,0:T(8,128)(2,1)S(1)}, f32[256,256]{1,0:T(8,128)S(1)}, f32[256,256]{1,0:T(8,128)S(1)}) custom-call(bf16[4,128,512]{2,1,0:T(8,128)(2,1)S(1)} %get-tuple-element.11.dq, bf16[4,8,128,256]{3,2,1,0:T(8,128)(2,1)} %get-tuple-element.12.dkv, bf16[1,128,4096]{2,1,0:T(8,128)(2,1)} %tok.3, s32[2,1,128,256]{3,2,1,0:T(8,128)S(1)} %copy-done), custom_call_target="tpu_custom_call" | custom-call | flops 1000000000 | bytes 16777216 | tf_op jit(solution)/shard_map/back/pallas_call | solution.py:778
  135.2 0.8 copy.14
  136.0 0.7 copy.15
  136.7 0.7 copy.16
Async XLA Ops:
  0.6 43.8 %copy-start.1 = (s32[32]{0:T(128)S(1)}, s32[32]{0:T(128)}, u32[]{:S(2)}) copy-start(s32[32]{0:T(128)} %order.1) | copy-start | bytes 388
  44.5 18.8 %copy-start = (s32[2,1,128,256]{3,2,1,0:T(8,128)S(1)}, s32[2,1,128,256]{3,2,1,0:T(8,128)}, u32[]{:S(2)}) copy-start(s32[2,1,128,256]{3,2,1,0:T(8,128)} %masks.1) | copy-start | bytes 786436

commit v7 on v6

--- a/solution.py
+++ b/solution.py
@@ -718,15 +718,15 @@
     a1[0].step(0)
     passed_on.append(pass_on(1))
     passed_on.append(pass_on(2))
+    b1[0].step(0)
     a1[0].step(1)
     for copy in passed_on[1] + passed_on[2]:
         copy.wait_recv()
     a1[1].step(0)
-    b1[0].step(0)
     b1[1].step(0)
     a1[0].step(2)
+    b1[0].step(1)
     a1[1].step(1)
-    b1[0].step(1)
     a1[0].step(3)
     a1[1].step(2)
     b1[1].step(1)

time: 138 us -> 139 us (level)
  Pallas kernels: 135 us -> 137 us
    pallas_call x1, Pallas kernels: 18.8 us -> 22.1 us  [attention(): pl.pallas_call(attention_kernel, name='attention', out_shape=(jax.ShapeDt...]
where the time goes in v7:
time: 139 us; the launch traced here: 140 us
  Pallas kernels  137 us (99%)
  local copies, waits for them, and re-layouts  2.21 us (2%)
    pallas_call x1, Pallas kernels, back(): pl.pallas_call(back_kernel, name='back', out_shape=(jax.ShapeDtypeStruct(...  70.7 us
    pallas_call x1, Pallas kernels, front(): pl.pallas_call(front_kernel, name='front', out_shape=(jax.ShapeDtypeStruc...  43.8 us
    pallas_call x1, Pallas kernels, attention(): pl.pallas_call(attention_kernel, name='attention', out_shape=(jax.ShapeDt...  22.1 us

profile of v7, /device:TPU:71, one launch (start us, length us, event | category | flops | bytes accessed | tf_op | source)
XLA Modules:
  0.0 139.5 jit_solution(3368357602640711002)
XLA Ops:
  0.6 0.0 copy-start.1
  0.6 43.8 %front.1 = (bf16[4,128,512]{2,1,0:T(8,128)(2,1)}, bf16[4,128,512]{2,1,0:T(8,128)(2,1)}, bf16[32,128,256]{2,1,0:T(8,128)(2,1)}) custom-call(bf16[1,128,4096]{2,1,0:T(8,128)(2,1)} %tok.3, bf16[1,128,2048]{2,1,0:T(8,128)(2,1)} %q.1, bf16[1,128,2048]{2,1,0:T(8,128)(2,1)} %do.1, bf16[8192,256]{1,0:T(8,128)(2,1)} %kw.1, bf16[8192,256]{1,0:T(8,128)(2,1)} %vw.1, ...), custom_call_target="tpu_custom_call" | custom-call | flops 1000000000 | bytes 16777216 | tf_op jit(solution)/shard_map/front/pallas_call | solution.py:220
  44.5 0.0 copy-done.1
  44.5 0.0 copy-start
  44.5 22.1 %attention.1 = (bf16[4,128,512]{2,1,0:T(8,128)(2,1)S(1)}, bf16[4,8,128,256]{3,2,1,0:T(8,128)(2,1)}) custom-call(s32[32]{0:T(128)S(1)} %copy-done.1, bf16[4,128,512]{2,1,0:T(8,128)(2,1)} %get-tuple-element.8.q, bf16[4,128,512]{2,1,0:T(8,128)(2,1)} %get-tuple-element.9.do, bf16[32,128,256]{2,1,0:T(8,128)(2,1)} %get-tuple-element.10.kv), custom_call_target="tpu_custom_call" | custom-call | flops 10000000000 | bytes 8388608 | tf_op jit(solution)/shard_map/attention/pallas_call | solution.py:379
  66.6 0.0 copy-done
  66.6 70.7 %back.1 = (bf16[1,128,2048]{2,1,0:T(8,128)(2,1)S(1)}, f32[256,256]{1,0:T(8,128)S(1)}, f32[256,256]{1,0:T(8,128)S(1)}) custom-call(bf16[4,128,512]{2,1,0:T(8,128)(2,1)S(1)} %get-tuple-element.11.dq, bf16[4,8,128,256]{3,2,1,0:T(8,128)(2,1)} %get-tuple-element.12.dkv, bf16[1,128,4096]{2,1,0:T(8,128)(2,1)} %tok.3, s32[2,1,128,256]{3,2,1,0:T(8,128)S(1)} %copy-done), custom_call_target="tpu_custom_call" | custom-call | flops 1000000000 | bytes 16777216 | tf_op jit(solution)/shard_map/back/pallas_call | solution.py:778
  137.3 0.8 copy.14
  138.1 0.7 copy.15
  138.8 0.7 copy.16
Async XLA Ops:
  0.6 43.8 %copy-start.1 = (s32[32]{0:T(128)S(1)}, s32[32]{0:T(128)}, u32[]{:S(2)}) copy-start(s32[32]{0:T(128)} %order.1) | copy-start | bytes 388
  44.5 22.1 %copy-start = (s32[2,1,128,256]{3,2,1,0:T(8,128)S(1)}, s32[2,1,128,256]{3,2,1,0:T(8,128)}, u32[]{:S(2)}) copy-start(s32[2,1,128,256]{3,2,1,0:T(8,128)} %masks.1) | copy-start | bytes 786436
